TPU v7x, 32 devices: a whole 2x2x4 slice. The times are simulated.
32 devices in a mesh: expert: 2 (over x), tensor: 16 (over z, y, core).
Axes of the slice: x: 2, y: 2, z: 4, core: 2. Of those that a mesh axis runs over, the one named last changes fastest.
Arguments:
- tokens: bfloat16 [128, 6144], P(('expert', 'tensor')), may hold values from -6 to 6
- gate_weights: bfloat16 [128, 2], P(('expert', 'tensor')), may hold values from 0.19921875 to 1
- expert_ids: int32 [128, 2], P(('expert', 'tensor')), may hold values from 0 to 3, all different within a row; in each aligned block of 128 rows (0 to 127, 128 to 255, ...) at most 96 rows name the same one
- w_gate: bfloat16 [4, 6144, 16384], P('expert', None, 'tensor'), may hold values from -0.078125 to 0.078125
- w_up: bfloat16 [4, 6144, 16384], P('expert', None, 'tensor'), may hold values from -0.078125 to 0.078125
- w_down: bfloat16 [4, 16384, 6144], P('expert', 'tensor'), may hold values from -0.046875 to 0.046875
Outputs:
- mixed: bfloat16 [128, 6144], P(('expert', 'tensor'))
Inputs may be any that keep to these rules, and one draw needn't show every extreme that they name: `expert_ids`: the 2 ids of a token differ; every expert is named by at most 96 tokens, a bound that some block reaches.
All inputs are finite; a program needn't handle non-finite values.
Results may differ from a plain program's by a relative error of at most 0.0049.
Values may be sent and summed in bfloat16 or wider, within the bound.
No kernel may reach another device: no remote copies, remote signals or barrier semaphores. Data moves between devices by JAX's collectives and lax.ppermute only.
A program may use at most 192 MiB of HBM per device.

v0:
```python
import jax
import jax.numpy as jnp
from jax import lax
from jax.sharding import PartitionSpec as P


def routing_lists(expert_ids, gate_weights, expert, capacity):
    matches = expert_ids == expert
    chosen = jnp.any(matches, axis=1)
    weight = jnp.sum(jnp.where(matches, gate_weights.astype(jnp.float32), jnp.float32(0.0)), axis=1)
    ranking = jnp.cumsum(chosen.astype(jnp.int32)) - 1
    target = jnp.where(chosen, ranking, capacity)
    token_count = expert_ids.shape[0]
    slot_tok = (
        jnp.full((capacity,), token_count, jnp.int32)
        .at[target]
        .set(jnp.arange(token_count, dtype=jnp.int32), mode="drop")
    )
    slot_gate = jnp.zeros((capacity,), jnp.float32).at[target].set(weight, mode="drop")
    slot_count = jnp.sum(chosen.astype(jnp.int32))
    return (slot_tok, slot_gate, slot_count)


def expert_rows(slot_rows, gate_mat, up_mat, down_mat):
    gate_proj = jnp.dot(slot_rows, gate_mat, preferred_element_type=jnp.float32)
    up_proj = jnp.dot(slot_rows, up_mat, preferred_element_type=jnp.float32)
    hidden = (jax.nn.silu(gate_proj) * up_proj).astype(jnp.bfloat16)
    return jnp.dot(hidden, down_mat, preferred_element_type=jnp.float32)


def place_rows(values, positions, first_row, row_count):
    inside = (positions >= first_row) & (positions < first_row + row_count)
    target = jnp.where(inside, positions, row_count)
    table = jnp.zeros((row_count, values.shape[1]), jnp.float32)
    return table.at[target].add(values, mode="drop")


def shards(tokens, gate_weights, expert_ids, w_gate, w_up, w_down):
    all_tokens, all_gates = (
        lax.all_gather(tokens, ("expert", "tensor"), axis=0, tiled=True),
        lax.all_gather(gate_weights, ("expert", "tensor"), axis=0, tiled=True),
    )
    all_ids = lax.all_gather(expert_ids, ("expert", "tensor"), axis=0, tiled=True)
    token_count = all_tokens.shape[0]
    local_count = w_gate.shape[0]
    capacity = 3 * token_count // 4
    group_index = lax.axis_index("expert")
    weighted_list = []
    place_list = []
    for local_expert in range(local_count):
        expert = group_index * local_count + local_expert
        slot_tok, slot_gate, slot_count = routing_lists(all_ids, all_gates, expert, capacity)
        slot_rows = all_tokens[jnp.minimum(slot_tok, token_count - 1)]
        expert_out = expert_rows(
            slot_rows, w_gate[local_expert], w_up[local_expert], w_down[local_expert]
        )
        weighted = expert_out * slot_gate[:, None]
        weighted_list.append(weighted)
        place_list.append(slot_tok)
    values = jnp.concatenate(weighted_list, axis=0)
    places = jnp.concatenate(place_list, axis=0)
    n_tensor = lax.axis_size("tensor")
    n_expert = lax.axis_size("expert")
    tok_dev = token_count // (n_tensor * n_expert)
    summed = lax.psum_scatter(
        place_rows(values, places, jnp.int32(0), tok_dev * lax.axis_size(("expert", "tensor"))),
        ("expert", "tensor"),
        scatter_dimension=0,
        tiled=True,
    )
    return summed.astype(jnp.bfloat16)


def solution(mesh):
    in_specs = (
        P(("expert", "tensor"), None),
        P(("expert", "tensor"), None),
        P(("expert", "tensor"), None),
        P("expert", None, "tensor"),
        P("expert", None, "tensor"),
        P("expert", "tensor", None),
    )
    out_specs = P(("expert", "tensor"), None)
    return jax.shard_map(shards, mesh=mesh, in_specs=in_specs, out_specs=out_specs, check_vma=False)
```

profile of v0, /device:TPU:0, one launch (start us, length us, event | category | flops | bytes accessed | tf_op | source)
XLA Modules:
  0.0 230.1 jit_solution(14295730270843726631)
XLA Ops:
  6.5 0.0 all-gather.5.cloned.1.call-start
  6.5 0.7 all-gather.5.cloned.1.call-update
  7.3 43.5 %all-gather = s32[32,4,2]{1,2,0:T(2,128)S(1)} all-gather(s32[1,4,2]{1,2,0:T(2,128)} %bitcast.45), channel_id=1, replica_groups=mesh['expert'=2,'tensor'=16] {'expert','tensor'}, dimensions={0}, use_global_device_ids=true | all-gather | bytes 1056 | tf_op jit(solution)/shard_map/all_gather | solution.py:43
  50.8 0.1 fusion.61
  50.9 0.1 reduce_or.23
  51.0 0.1 copy.16
  51.1 0.1 reduce_or.25
  51.3 0.1 copy.18
  51.4 0.1 copy.15
  51.5 36.6 %all-gather.2 = bf16[32,4,2]{1,2,0:T(2,128)(2,1)S(1)} all-gather(bf16[1,4,2]{1,2,0:T(2,128)(2,1)} %bitcast.47), channel_id=1, replica_groups=mesh['expert'=2,'tensor'=16] {'expert','tensor'}, dimensions={0}, use_global_device_ids=true | all-gather | bytes 528 | tf_op jit(solution)/shard_map/all_gather | solution.py:41
  88.1 0.1 fusion.60
  88.2 0.1 reshape.236
  88.3 0.1 copy.17
  88.5 0.2 reduce-window.6
  88.6 0.2 reduce-window.9
  88.8 0.1 reshape.237
  88.9 0.1 fusion.57
  89.0 1.0 scatter_custom_fusion.2
  90.0 1.0 scatter_custom_fusion
  91.0 0.1 fusion.58
  91.1 1.0 scatter_custom_fusion.3
  92.1 1.0 scatter_custom_fusion.1
  93.1 0.1 compare_select_fusion.2
  93.2 0.0 all-gather.5.cloned.1.call-done
  93.3 2.7 %reshape.220 = bf16[128,6144]{1,0:T(8,128)(2,1)S(1)} reshape(bf16[32,4,6144]{2,1,0:T(4,128)(2,1)} %all-gather.5.cloned.1.call-done) | data formatting | bytes 3145728
  96.0 2.3 gather_fusion
  98.2 1.3 gather_fusion.1
  99.5 6.1 %fusion.10 = f32[96,1024]{1,0:T(8,128)S(1)} fusion(bf16[96,6144]{1,0:T(8,128)(2,1)} %gather_fusion, bf16[2,6144,1024]{2,1,0:T(8,128)(2,1)} %param.9), kind=kOutput, calls=%fused_computation.17 | convolution fusion | flops 1207959552 | bytes 14155776 | tf_op jit(solution)/shard_map/dot_general | solution.py:25
  105.6 0.0 copy-start
  105.6 5.8 %fusion.4 = f32[96,1024]{1,0:T(8,128)S(1)} fusion(bf16[96,6144]{1,0:T(8,128)(2,1)S(1)} %gather_fusion.1, bf16[2,6144,1024]{2,1,0:T(8,128)(2,1)} %param.9), kind=kOutput, calls=%fused_computation.11 | convolution fusion | flops 1207959552 | bytes 14155776 | tf_op jit(solution)/shard_map/dot_general | solution.py:25
  111.4 0.0 copy-done
  111.4 12.0 %fusion.18 = f32[96,6144]{1,0:T(8,128)} fusion(bf16[2,1024,6144]{2,1,0:T(8,128)(2,1)} %param.11, f32[96]{0:T(128)S(1)} %scatter_custom_fusion.2, bf16[96,6144]{1,0:T(8,128)(2,1)S(1)} %copy-done, bf16[2,6144,1024]{2,1,0:T(8,128)(2,1)} %param.10, f32[96,1024]{1,0:T(8,128)S(1)} %fusion.10), kind=kOutput, calls=%fused_computation.25 | convolution fusion | flops 2417098752 | bytes 29098368 | tf_op jit(solution)/shard_map/dot_general | solution.py:28
  123.5 12.0 %fusion.21 = f32[96,6144]{1,0:T(8,128)} fusion(bf16[2,1024,6144]{2,1,0:T(8,128)(2,1)} %param.11, f32[96]{0:T(128)S(1)} %scatter_custom_fusion.3, bf16[96,6144]{1,0:T(8,128)(2,1)S(1)} %gather_fusion.1, bf16[2,6144,1024]{2,1,0:T(8,128)(2,1)} %param.10, f32[96,1024]{1,0:T(8,128)S(1)} %fusion.4), kind=kOutput, calls=%fused_computation.26 | convolution fusion | flops 2417098752 | bytes 29098368 | tf_op jit(solution)/shard_map/dot_general | solution.py:28
  135.5 9.1 %scatter_custom_fusion.4 = f32[128,6144]{1,0:T(8,128)S(1)} fusion(s32[192]{0:T(256)S(1)} %bitcast.46, f32[96,6144]{1,0:T(8,128)} %fusion.21, f32[]{:T(128)} %constant.49, f32[96,6144]{1,0:T(8,128)} %fusion.18, f32[]{:T(128)} %constant.12.clone.1), kind=kCustom, calls=%fused_computation.27 | custom fusion | flops 2359296 | bytes 7864328 | tf_op jit(solution)/shard_map/scatter-add | solution.py:35
  144.6 77.1 %all-reduce.2 = bf16[128,6144]{1,0:T(8,128)(2,1)} all-reduce(f32[128,6144]{1,0:T(8,128)S(1)} %scatter_custom_fusion.4), channel_id=2, replica_groups=mesh['expert'=2,'tensor'=16] {'expert','tensor'}, use_global_device_ids=true, to_apply=%region_11.12.clone | all-reduce | flops 786432 | bytes 4718592
  221.7 1.5 dynamic-slice_convert_fusion
  (8 shorter events, 0.0 us)
Async XLA Ops:
  6.5 86.7 %all-gather.5.cloned.1.call-start = ((), (), s32[]{:S(2)}) async-start(), calls=%async_computation | async-start | bytes 1622016 | tf_op jit(solution)/shard_map/all_gather | solution.py:40
  105.6 5.9 %copy-start = (bf16[96,6144]{1,0:T(8,128)(2,1)S(1)}, bf16[96,6144]{1,0:T(8,128)(2,1)}, u32[]{:S(2)}) copy-start(bf16[96,6144]{1,0:T(8,128)(2,1)} %gather_fusion) | copy-start | bytes 3538948
Sparse Core Ops, SparseCore 0:
  10.2 57.7 all-gather.4
where the time goes:
time: 230 us
  blocking collectives  157 us (68%)
  matrix products  36 us (16%)
  between operations  13.6 us (6%)
  local copies, waits for them, and re-layouts  12.6 us (5%)
  other arithmetic  10 us (4%)
    unnamed x1, blocking collectives  77.1 us
    all_gather x1, blocking collectives, shards(): lax.all_gather(expert_ids, ('expert', 'tensor'), axis=0, tiled=True)  43.5 us
    all_gather x1, blocking collectives, shards(): lax.all_gather(gate_weights, ('expert', 'tensor'), axis=0, tiled=True)  36.6 us
    dot_general x2, matrix products, expert_rows(): return jnp.dot(hidden, down_mat, preferred_element_type=jnp.float32)  24 us
    dot_general x2, matrix products, expert_rows(): gate_proj = jnp.dot(slot_rows, gate_mat, preferred_element_type=jnp.float32)  11.9 us
    scatter-add x1, other arithmetic, place_rows(): return table.at[target].add(values, mode='drop')  9.14 us
  transfers between devices with their start and end apart: 1, of which 0 were waited for; matrix products, arithmetic and copies ran while one was open for 2% of the time, Pallas kernels for 0%

commit v1 on v0

v1 whole, which is shorter than its diff:
```python
import functools
import jax
import jax.numpy as jnp
from jax import lax
from jax.experimental import pallas as pl
from jax.experimental.pallas import tpu as pltpu
from jax.sharding import PartitionSpec as P

LANES = 128
BOTH = ("expert", "tensor")
VMEM = pl.BlockSpec(memory_space=pltpu.VMEM)
HBM = pl.BlockSpec(memory_space=pltpu.HBM)
MIB = 1 << 20
RING = 6


def exchange(x, ke, kt):
    ne, nt = lax.axis_size("expert"), lax.axis_size("tensor")
    pairs = [(e * nt + t, (e ^ ke) * nt + (t ^ kt)) for e in range(ne) for t in range(nt)]
    return lax.ppermute(x, BOTH, pairs)


def near_offsets():
    return [(e, y) for e in range(lax.axis_size("expert")) for y in (0, 2)][1:]


def far_offsets():
    return [(0, 4 * k) for k in range(1, lax.axis_size("tensor") // 4)]


def in_vmem(x):
    return pltpu.with_memory_space_constraint(x, pltpu.VMEM)


def unit_of(ref, spot):
    kind, e, half, h = spot
    return ref.at[e, :, pl.ds(half * h, h)] if kind == 2 else ref.at[e, pl.ds(half * h, h), :]


def stage(compute, weights, loads, deps, ins, outs, scratch, flops, limit):
    n_load, n_in = len(loads), len(ins)
    kinds = sorted({spot[0] for spot in loads})
    used = [weights[k] for k in kinds]
    e_count, d, f = weights[0].shape
    shapes = [(f, spot[3]) if spot[0] == 2 else (spot[3], f) for spot in loads]

    def kernel(*refs):
        refs = list(refs)
        hbm = {k: refs.pop(0) for k in kinds}
        del refs[: len(deps)]
        in_refs = [refs.pop(0) for _ in range(n_in)]
        unit_refs = [refs.pop(0) for _ in range(n_load)]
        token_ref = refs.pop(0)
        out_refs = [refs.pop(0) for _ in outs]
        sems = refs.pop() if n_load else None
        copies = [
            pltpu.make_async_copy(unit_of(hbm[spot[0]], spot), unit_refs[i], sems.at[i])
            for i, spot in enumerate(loads)
        ]
        for copy in copies:
            copy.start()
        token_ref[...] = jnp.zeros_like(token_ref)
        if compute is not None:
            compute(in_refs, out_refs, refs)
        for copy in copies:
            copy.wait()

    size = sum(2 * a * b for a, b in shapes)
    results = pl.pallas_call(
        kernel,
        in_specs=[HBM] * len(used) + [pl.BlockSpec(memory_space=pl.ANY)] * len(deps) + [VMEM] * n_in,
        out_specs=[VMEM] * (n_load + 1 + len(outs)),
        out_shape=[pltpu.VMEM(s, jnp.bfloat16) for s in shapes]
        + [pltpu.VMEM((8, LANES), jnp.float32)]
        + [pltpu.VMEM(s, t) for s, t in outs],
        scratch_shapes=list(scratch) + ([pltpu.SemaphoreType.DMA((n_load,))] if n_load else []),
        compiler_params=pltpu.CompilerParams(vmem_limit_bytes=limit),
        cost_estimate=pl.CostEstimate(flops=flops, bytes_accessed=size, transcendentals=0),
    )(*[pltpu.with_memory_space_constraint(w, pltpu.HBM) for w in used], *deps, *[in_vmem(x) for x in ins])
    return list(results[:n_load]), results[n_load], list(results[n_load + 1 :])


def columns(count, step, body):
    @pl.loop(0, count // step)
    def _(i):
        body(pl.ds(pl.multiple_of(i * step, step), step))


def dot(a, b):
    return jnp.dot(a, b, preferred_element_type=jnp.float32)


def shards(tokens, gate_weights, expert_ids, w_gate, w_up, w_down):
    weights = (w_gate, w_up, w_down)
    e_count, d, f = w_gate.shape
    ne, nt = lax.axis_size("expert"), lax.axis_size("tensor")
    own = tokens.shape[0]
    total = own * ne * nt
    half = d // 2
    fb = min(256, f)
    rows = own * (nt // 4)

    experts = lax.broadcasted_iota(jnp.int32, (1, LANES), 1)
    gates = sum(
        jnp.where(expert_ids[:, i : i + 1] == experts, gate_weights[:, i : i + 1], jnp.bfloat16(0))
        for i in range(expert_ids.shape[1])
    )
    packed = jnp.concatenate([gates, tokens], axis=1)

    def load_only(loads, *deps):
        units, token, _ = stage(None, weights, loads, deps, [], [], [], 0, 2 * MIB)
        return units, token

    last = e_count - 1
    resident = [(k, e, h, half) for e in range(last) for k in (0, 1) for h in (0, 1)]
    resident += [(0, last, 0, half), (1, last, 0, half)]
    cut = len(resident) // 2
    far = [exchange(packed, *k) for k in far_offsets()]
    units, token = load_only(resident[:cut], packed)
    block = jnp.concatenate([packed] + far, axis=0)
    block, token = lax.optimization_barrier((block, token))
    pieces = [block] + [exchange(block, *k) for k in near_offsets()]
    more, token = load_only(resident[cut:], block, token)
    pieces[-1], token = lax.optimization_barrier((pieces[-1], token))
    units = units + more
    pieces = pieces + [exchange(p, 0, 1) for p in pieces]

    chunk = 1024
    n_k, n_d = half // chunk, d // chunk
    stream = [(k, j) for j in range(n_k) for k in (0, 1)]
    stream += [(2 + e, j) for j in range(n_d) for e in range(e_count)]
    slots = RING

    def kernel(*refs):
        refs = list(refs)
        wg, wu, wd = refs[:3]
        del refs[:4]
        xrefs = [refs.pop(0) for _ in pieces]
        held = {spot[:3]: refs.pop(0) for spot in resident}
        sends = [refs.pop(0) for _ in range(2)]
        keeps = [refs.pop(0) for _ in range(2)]
        xs, gate_ref, g_ref, u_ref, h_ref, ring, sems = refs

        def slot(i):
            kind, j = stream[i]
            view = ring.at[i % slots]
            return view.at[:chunk, :f] if kind < 2 else view.at[:f, :chunk]

        def copy(i):
            kind, j = stream[i]
            if kind < 2:
                src = (wg, wu)[kind].at[last, pl.ds(half + j * chunk, chunk), :]
            else:
                src = wd.at[kind - 2, :, pl.ds(j * chunk, chunk)]
            return pltpu.make_async_copy(src, slot(i), sems.at[i % slots])

        for i in range(slots):
            copy(i).start()

        me = lax.axis_index("expert")
        for i, ref in enumerate(xrefs):
            r = slice(i * rows, (i + 1) * rows)
            xs[r, :] = ref[:, LANES:]
            meta = ref[:, :LANES].astype(jnp.float32)
            lane = lax.broadcasted_iota(jnp.int32, meta.shape, 1)
            for e in range(e_count):
                col = jnp.sum(jnp.where(lane == me * e_count + e, meta, 0.0), axis=1, keepdims=True)
                gate_ref[e, r, :] = jnp.broadcast_to(col, meta.shape)

        def hide(e, c, g, u):
            h_ref[e, :, c] = (g / (1.0 + jnp.exp(-g)) * u).astype(jnp.bfloat16)

        def begin(c):
            g_ref[:, c] = dot(xs[:, :half], held[0, last, 0][:, c])
            u_ref[:, c] = dot(xs[:, :half], held[1, last, 0][:, c])

        columns(f, fb, begin)
        for j in range(n_k):
            k = slice(half + j * chunk, half + (j + 1) * chunk)
            sg, su = slot(2 * j), slot(2 * j + 1)
            copy(2 * j).wait()
            copy(2 * j + 1).wait()

            def add(c):
                g = g_ref[:, c] + dot(xs[:, k], sg[:, c])
                u = u_ref[:, c] + dot(xs[:, k], su[:, c])
                if j < n_k - 1:
                    g_ref[:, c] = g
                    u_ref[:, c] = u
                else:
                    hide(last, c, g, u)

            columns(f, fb, add)
            for i in (2 * j, 2 * j + 1):
                if i + slots < len(stream):
                    copy(i + slots).start()
        for e in range(last):

            def whole(c):
                g = dot(xs[:, :half], held[0, e, 0][:, c]) + dot(xs[:, half:], held[0, e, 1][:, c])
                u = dot(xs[:, :half], held[1, e, 0][:, c]) + dot(xs[:, half:], held[1, e, 1][:, c])
                hide(e, c, g, u)

            columns(f, fb, whole)
        for j in range(n_d):
            at = [2 * n_k + j * e_count + e for e in range(e_count)]
            views = [slot(i) for i in at]
            for i in at:
                copy(i).wait()
            side, start = divmod(j * chunk, half)

            def out(c):
                s = sum(dot(h_ref[e], views[e][:, c]) * gate_ref[e, :, 0:1] for e in range(e_count))
                to = pl.ds(pl.multiple_of(c.start + start, 256), 256)
                keeps[side][:, to] = s[: total // 2]
                sends[side][:, to] = s[total // 2 :].astype(jnp.bfloat16)

            columns(chunk, 256, out)
            for i in at:
                if i + slots < len(stream):
                    copy(i + slots).start()

    side_len = max(chunk, f)
    scratch = 2 * total * d + 4 * e_count * total * LANES + 8 * total * f + 2 * e_count * total * f
    scratch += 2 * slots * side_len * side_len
    ins = pieces + units
    results = pl.pallas_call(
        kernel,
        in_specs=[HBM] * 3 + [pl.BlockSpec(memory_space=pl.ANY)] + [VMEM] * len(ins),
        out_specs=[VMEM] * 4,
        out_shape=[pltpu.VMEM((total // 2, half), jnp.bfloat16)] * 2
        + [pltpu.VMEM((total // 2, half), jnp.float32)] * 2,
        scratch_shapes=[
            pltpu.VMEM((total, d), jnp.bfloat16),
            pltpu.VMEM((e_count, total, LANES), jnp.float32),
            pltpu.VMEM((total, f), jnp.float32),
            pltpu.VMEM((total, f), jnp.float32),
            pltpu.VMEM((e_count, total, f), jnp.bfloat16),
            pltpu.VMEM((slots, side_len, side_len), jnp.bfloat16),
            pltpu.SemaphoreType.DMA((slots,)),
        ],
        compiler_params=pltpu.CompilerParams(vmem_limit_bytes=-(-scratch // MIB) * MIB),
        cost_estimate=pl.CostEstimate(
            flops=6 * total * d * f * e_count, bytes_accessed=4 * d * f * e_count, transcendentals=0
        ),
    )(*[pltpu.with_memory_space_constraint(w, pltpu.HBM) for w in weights], token, *[in_vmem(x) for x in ins])

    sums = []
    for send, keep in zip(results[:2], results[2:]):
        s = keep + exchange(send, 0, 1).astype(jnp.float32)
        got = [
            exchange(s[i * rows : (i + 1) * rows].astype(jnp.bfloat16), *k)
            for i, k in enumerate(near_offsets(), 1)
        ]
        sums.append(s[:rows] + sum(g.astype(jnp.float32) for g in got))
    s = jnp.concatenate(sums, axis=1)
    got = [
        exchange(s[i * own : (i + 1) * own].astype(jnp.bfloat16), *k)
        for i, k in enumerate(far_offsets(), 1)
    ]
    s = s[:own] + sum(g.astype(jnp.float32) for g in got)
    return s.astype(jnp.bfloat16)


def solution(mesh):
    in_specs = (
        P(("expert", "tensor"), None),
        P(("expert", "tensor"), None),
        P(("expert", "tensor"), None),
        P("expert", None, "tensor"),
        P("expert", None, "tensor"),
        P("expert", "tensor", None),
    )
    out_specs = P(("expert", "tensor"), None)
    return jax.shard_map(shards, mesh=mesh, in_specs=in_specs, out_specs=out_specs, check_vma=False)
```

time: 230 us -> 72.8 us (0.32)
  blocking collectives: 157 us -> 0 us
  matrix products: 36 us -> 0 us
  Pallas kernels: 0 us -> 32.5 us
  starting transfers between devices: 0.01 us -> 22.4 us
  between operations: 13.6 us -> 0.17 us
  waiting for transfers between devices: 0.73 us -> 13.9 us
  local copies, waits for them, and re-layouts: 12.6 us -> 1.61 us
  other arithmetic: 10 us -> 1.99 us
    all_gather x2 -> x0, blocking collectives: 80.1 us -> none  [the longest x1 43.5 us: shards(): lax.all_gather(expert_ids, ('expert', 'tensor'), axis=0, tiled=True)]
    unnamed x1 -> x0, blocking collectives: 77.1 us -> none
    dot_general x4 -> x0, matrix products: 36 us -> none  [the longest x2 24 us: expert_rows(): return jnp.dot(hidden, down_mat, preferred_element_type=jnp.float32)]
    pallas_call x0 -> x3, Pallas kernels: none -> 32.5 us  [the longest x1 19.6 us: shards(): pl.pallas_call(kernel, in_specs=[HBM] * 3 + [pl.BlockSpec(memory_space=pl...]
    ppermute x0 -> x21, starting transfers between devices: none -> 22.4 us  [exchange(): return lax.ppermute(x, BOTH, pairs)]
    ppermute x0 -> x21, waiting for transfers between devices: none -> 13.9 us  [exchange(): return lax.ppermute(x, BOTH, pairs)]
    scatter-add x1 -> x0, other arithmetic: 9.14 us -> none  [place_rows(): return table.at[target].add(values, mode='drop')]
    scatter x4 -> x0, local copies, waits for them, and re-layouts: 3.92 us -> none  [the longest x2 1.97 us: routing_lists(): jnp.zeros((capacity,), jnp.float32).at[target].set(weight, mode='drop')]
  transfers between devices with their start and end apart: 1 -> 21, of which waited for: 0 -> 13; matrix products, arithmetic and copies ran while one was open for 2% -> 0% of each run, Pallas kernels for 0% -> 18%
where the time goes in v1:
time: 72.8 us; the launch traced here: 72.6 us
  Pallas kernels  32.5 us (45%)
  starting transfers between devices  22.4 us (31%)
  waiting for transfers between devices  13.9 us (19%)
  other arithmetic  1.99 us (3%)
  local copies, waits for them, and re-layouts  1.61 us (2%)
    ppermute x21, starting transfers between devices, exchange(): return lax.ppermute(x, BOTH, pairs)  22.4 us
    pallas_call x1, Pallas kernels, shards(): pl.pallas_call(kernel, in_specs=[HBM] * 3 + [pl.BlockSpec(memory_space=pl...  19.6 us
    ppermute x21, waiting for transfers between devices, exchange(): return lax.ppermute(x, BOTH, pairs)  13.9 us
    pallas_call x2, Pallas kernels, stage(): pl.pallas_call(kernel, in_specs=[HBM] * len(used) + [pl.BlockSpec(memory_...  12.8 us
  transfers between devices with their start and end apart: 21, of which 13 were waited for; matrix products, arithmetic and copies ran while one was open for 0% of the time, Pallas kernels for 18%

profile of v1, /device:TPU:0, one launch (start us, length us, event | category | flops | bytes accessed | tf_op | source)
XLA Modules:
  0.0 72.6 jit_solution(3188052549925289439)
XLA Ops:
  0.0 0.7 %slice_bitcast_fusion.2 = (bf16[4]{0:T(256)(128)(2,1)S(1)}, bf16[4]{0:T(256)(128)(2,1)S(1)}) fusion(bf16[4,2]{0,1:T(2,128)(2,1)} %param.7), kind=kLoop, calls=%fused_computation.20 | loop fusion | bytes 32 | tf_op jit(solution)/shard_map/jit(_where)/broadcast_in_dim | solution.py:105
  0.7 0.8 %slice_bitcast_fusion.3 = (s32[4]{0:T(128)S(1)}, s32[4]{0:T(128)S(1)}) fusion(s32[4,2]{0,1:T(2,128)} %param.8), kind=kLoop, calls=%fused_computation.21 | loop fusion | bytes 64 | tf_op jit(solution)/shard_map/eq | solution.py:105
  1.5 0.1 fusion.6
  1.6 0.8 %pad_maximum_fusion.2.refs_2_ = bf16[4,6272]{1,0:T(4,128)(2,1)S(1)} fusion(bf16[4,6144]{1,0:T(4,128)(2,1)} %param.6, bf16[4,128]{1,0:T(4,128)(2,1)S(1)} %fusion.6), kind=kLoop, calls=%fused_computation.12 | loop fusion | flops 100352 | bytes 100352 | tf_op jit(solution)/shard_map/concatenate | solution.py:108
  2.4 0.0 copy-start.1
  2.4 5.1 %collective-permute-start.2 = (bf16[4,6272]{1,0:T(4,128)(2,1)S(1)}, bf16[4,6272]{1,0:T(4,128)(2,1)S(1)}, u32[]{:S(2)}, u32[]{:S(2)}) collective-permute-start(bf16[4,6272]{1,0:T(4,128)(2,1)S(1)} %pad_maximum_fusion.2.refs_2_), channel_id=1, source_target_pairs={{0,12},{1,13},{2,14},{3,15},{4,8},{5,9},{6,10},{7,11},{8,4},{9,5},... | collective-permute-start | bytes 150536 | tf_op jit(solution)/shard_map/ppermute | solution.py:20
  7.5 0.0 collective-permute-start.1
  7.5 0.6 collective-permute-start
  8.2 6.4 %shard_map.64 = (bf16[3072,1024]{1,0:T(8,128)(2,1)S(1)}, bf16[3072,1024]{1,0:T(8,128)(2,1)S(1)}, bf16[3072,1024]{1,0:T(8,128)(2,1)S(1)}, f32[8,128]{1,0:T(8,128)S(1)}) custom-call(bf16[2,6144,1024]{2,1,0:T(8,128)(2,1)} %refs_0_.5, bf16[2,6144,1024]{2,1,0:T(8,128)(2,1)} %refs_1_.5, bf16[4,6272]{1,0:T(4,128)(2,1)S(1)} %pad_maximum_fusion.2.refs_2_), custom_call_target="tpu_custom_call" | custom-call | bytes 18874368 | tf_op jit(solution)/shard_map/pallas_call | solution.py:69
  14.6 0.0 collective-permute-done.2
  14.6 0.0 collective-permute-done.1
  14.6 0.0 collective-permute-done
  14.6 0.0 copy-done.1
  14.6 0.1 pad_maximum_fusion.1.refs_2_.refs_4_
  14.8 2.7 %collective-permute-start.3 = (bf16[16,6272]{1,0:T(8,128)(2,1)S(1)}, bf16[16,6272]{1,0:T(8,128)(2,1)S(1)}, u32[]{:S(2)}, u32[]{:S(2)}) collective-permute-start(bf16[16,6272]{1,0:T(8,128)(2,1)S(1)} %pad_maximum_fusion.1.refs_2_.refs_4_), channel_id=1, source_target_pairs={{0,18},{1,19},{2,16},{3,17},{4,22},{5,23},{6,20},{7,21},{8,26},{9,... | collective-permute-start | bytes 602120 | tf_op jit(solution)/shard_map/ppermute | solution.py:20
  17.4 0.5 collective-permute-start.5
  18.0 0.4 collective-permute-start.4
  18.3 0.0 collective-permute-start.6
  18.3 6.4 %shard_map.65 = (bf16[3072,1024]{1,0:T(8,128)(2,1)S(1)}, bf16[3072,1024]{1,0:T(8,128)(2,1)S(1)}, bf16[3072,1024]{1,0:T(8,128)(2,1)S(1)}, f32[8,128]{1,0:T(8,128)S(1)}) custom-call(bf16[2,6144,1024]{2,1,0:T(8,128)(2,1)} %refs_0_.5, bf16[2,6144,1024]{2,1,0:T(8,128)(2,1)} %refs_1_.5, bf16[16,6272]{1,0:T(8,128)(2,1)S(1)} %pad_maximum_fusion.1.refs_2_.refs_4_, ...), custom_call_target="tpu_custom_call" | custom-call | bytes 18874368 | tf_op jit(solution)/shard_map/pallas_call | solution.py:69
  24.8 0.0 copy-start
  24.8 0.0 collective-permute-done.3.refs_7_
  24.8 1.5 %collective-permute-done.5.refs_6_ = bf16[16,6272]{1,0:T(8,128)(2,1)S(1)} collective-permute-done((bf16[16,6272]{1,0:T(8,128)(2,1)S(1)}, bf16[16,6272]{1,0:T(8,128)(2,1)S(1)}, u32[]{:S(2)}, u32[]{:S(2)}) %collective-permute-start.5) | collective-permute-done | bytes 200736 | tf_op jit(solution)/shard_map/ppermute | solution.py:20
  26.3 0.0 collective-permute-start.8
  26.3 0.0 collective-permute-done.4.refs_5_
  26.3 0.5 collective-permute-start.7
  26.8 0.0 collective-permute-start.9
  26.8 0.0 collective-permute-done.6.refs_8_
  26.8 0.9 %collective-permute-done.8.refs_10_ = bf16[16,6272]{1,0:T(8,128)(2,1)S(1)} collective-permute-done((bf16[16,6272]{1,0:T(8,128)(2,1)S(1)}, bf16[16,6272]{1,0:T(8,128)(2,1)S(1)}, u32[]{:S(2)}, u32[]{:S(2)}) %collective-permute-start.8) | collective-permute-done | bytes 200736 | tf_op jit(solution)/shard_map/ppermute | solution.py:20
  27.8 0.3 collective-permute-done.7.refs_9_
  28.0 0.3 collective-permute-done.9.refs_11_
  28.3 0.0 copy-done
  28.3 19.6 %shard_map.66 = (bf16[64,3072]{1,0:T(8,128)(2,1)S(1)}, bf16[64,3072]{1,0:T(8,128)(2,1)S(1)}, f32[64,3072]{1,0:T(8,128)S(1)}, f32[64,3072]{1,0:T(8,128)S(1)}) custom-call(bf16[2,6144,1024]{2,1,0:T(8,128)(2,1)} %refs_0_.5, bf16[2,6144,1024]{2,1,0:T(8,128)(2,1)} %refs_1_.5, bf16[2,1024,6144]{2,1,0:T(8,128)(2,1)} %refs_2_.1, f32[8,128]{1,0:T(8,128)} %copy-done, ...), custom_call_target="tpu_custom_call" | custom-call | flops 9663676416 | bytes 50331648 | tf_op jit(solution)/shard_map/pallas_call | solution.py:227
  48.0 0.3 collective-permute-start.10
  48.3 0.3 collective-permute-start.14
  48.5 1.2 %collective-permute-done.10 = bf16[64,3072]{1,0:T(8,128)(2,1)S(1)} collective-permute-done((bf16[64,3072]{1,0:T(8,128)(2,1)S(1)}, bf16[64,3072]{1,0:T(8,128)(2,1)S(1)}, u32[]{:S(2)}, u32[]{:S(2)}) %collective-permute-start.10) | collective-permute-done | bytes 393248 | tf_op jit(solution)/shard_map/ppermute | solution.py:20
  49.7 0.1 fusion.8
  49.9 1.2 %collective-permute-start.11 = (bf16[16,3072]{1,0:T(8,128)(2,1)S(1)}, bf16[16,3072]{1,0:T(8,128)(2,1)S(1)}, u32[]{:S(2)}, u32[]{:S(2)}) collective-permute-start(bf16[16,3072]{1,0:T(8,128)(2,1)S(1)} %get-tuple-element.44), channel_id=1, source_target_pairs={{0,2},{1,3},{2,0},{3,1},{4,6},{5,7},{6,4},{7,5},{8,10},{9,11},{10,... | collective-permute-start | bytes 294920 | tf_op jit(solution)/shard_map/ppermute | solution.py:20
  51.1 1.8 %collective-permute-start.13 = (bf16[16,3072]{1,0:T(8,128)(2,1)S(1)}, bf16[16,3072]{1,0:T(8,128)(2,1)S(1)}, u32[]{:S(2)}, u32[]{:S(2)}) collective-permute-start(bf16[16,3072]{1,0:T(8,128)(2,1)S(1)} %get-tuple-element.45), channel_id=1, source_target_pairs={{0,18},{1,19},{2,16},{3,17},{4,22},{5,23},{6,20},{7,21},{8,26},{9,... | collective-permute-start | bytes 294920 | tf_op jit(solution)/shard_map/ppermute | solution.py:20
  52.9 0.5 collective-permute-start.12
  53.4 0.0 collective-permute-done.14
  53.4 0.1 fusion.7
  53.6 1.2 %collective-permute-start.15 = (bf16[16,3072]{1,0:T(8,128)(2,1)S(1)}, bf16[16,3072]{1,0:T(8,128)(2,1)S(1)}, u32[]{:S(2)}, u32[]{:S(2)}) collective-permute-start(bf16[16,3072]{1,0:T(8,128)(2,1)S(1)} %get-tuple-element.41), channel_id=1, source_target_pairs={{0,2},{1,3},{2,0},{3,1},{4,6},{5,7},{6,4},{7,5},{8,10},{9,11},{10,... | collective-permute-start | bytes 294920 | tf_op jit(solution)/shard_map/ppermute | solution.py:20
  54.8 1.8 %collective-permute-start.17 = (bf16[16,3072]{1,0:T(8,128)(2,1)S(1)}, bf16[16,3072]{1,0:T(8,128)(2,1)S(1)}, u32[]{:S(2)}, u32[]{:S(2)}) collective-permute-start(bf16[16,3072]{1,0:T(8,128)(2,1)S(1)} %get-tuple-element.42), channel_id=1, source_target_pairs={{0,18},{1,19},{2,16},{3,17},{4,22},{5,23},{6,20},{7,21},{8,26},{9,... | collective-permute-start | bytes 294920 | tf_op jit(solution)/shard_map/ppermute | solution.py:20
  56.6 0.2 collective-permute-done.11
  56.8 1.4 %collective-permute-start.16 = (bf16[16,3072]{1,0:T(8,128)(2,1)S(1)}, bf16[16,3072]{1,0:T(8,128)(2,1)S(1)}, u32[]{:S(2)}, u32[]{:S(2)}) collective-permute-start(bf16[16,3072]{1,0:T(8,128)(2,1)S(1)} %get-tuple-element.43), channel_id=1, source_target_pairs={{0,16},{1,17},{2,18},{3,19},{4,20},{5,21},{6,22},{7,23},{8,24},{9,... | collective-permute-start | bytes 294920 | tf_op jit(solution)/shard_map/ppermute | solution.py:20
  58.1 0.0 collective-permute-done.13
  58.1 1.0 %collective-permute-done.12 = bf16[16,3072]{1,0:T(8,128)(2,1)S(1)} collective-permute-done((bf16[16,3072]{1,0:T(8,128)(2,1)S(1)}, bf16[16,3072]{1,0:T(8,128)(2,1)S(1)}, u32[]{:S(2)}, u32[]{:S(2)}) %collective-permute-start.12) | collective-permute-done | bytes 98336 | tf_op jit(solution)/shard_map/ppermute | solution.py:20
  59.2 1.4 %collective-permute-done.15 = bf16[16,3072]{1,0:T(8,128)(2,1)S(1)} collective-permute-done((bf16[16,3072]{1,0:T(8,128)(2,1)S(1)}, bf16[16,3072]{1,0:T(8,128)(2,1)S(1)}, u32[]{:S(2)}, u32[]{:S(2)}) %collective-permute-start.15) | collective-permute-done | bytes 98336 | tf_op jit(solution)/shard_map/ppermute | solution.py:20
  60.6 1.2 %collective-permute-done.17 = bf16[16,3072]{1,0:T(8,128)(2,1)S(1)} collective-permute-done((bf16[16,3072]{1,0:T(8,128)(2,1)S(1)}, bf16[16,3072]{1,0:T(8,128)(2,1)S(1)}, u32[]{:S(2)}, u32[]{:S(2)}) %collective-permute-start.17) | collective-permute-done | bytes 98336 | tf_op jit(solution)/shard_map/ppermute | solution.py:20
  61.8 0.6 collective-permute-done.16
  62.5 0.1 fusion.11
  62.6 1.5 %collective-permute-start.18 = (bf16[4,6144]{1,0:T(4,128)(2,1)S(1)}, bf16[4,6144]{1,0:T(4,128)(2,1)S(1)}, u32[]{:S(2)}, u32[]{:S(2)}) collective-permute-start(bf16[4,6144]{1,0:T(4,128)(2,1)S(1)} %get-tuple-element.47), channel_id=1, source_target_pairs={{0,4},{1,5},{2,6},{3,7},{4,0},{5,1},{6,2},{7,3},{8,12},{9,13},{10,... | collective-permute-start | bytes 147464 | tf_op jit(solution)/shard_map/ppermute | solution.py:20
  64.0 2.4 %collective-permute-start.20 = (bf16[4,6144]{1,0:T(4,128)(2,1)S(1)}, bf16[4,6144]{1,0:T(4,128)(2,1)S(1)}, u32[]{:S(2)}, u32[]{:S(2)}) collective-permute-start(bf16[4,6144]{1,0:T(4,128)(2,1)S(1)} %get-tuple-element.48), channel_id=1, source_target_pairs={{0,12},{1,13},{2,14},{3,15},{4,8},{5,9},{6,10},{7,11},{8,4},{9,5},... | collective-permute-start | bytes 147464 | tf_op jit(solution)/shard_map/ppermute | solution.py:20
  66.4 0.3 collective-permute-start.19
  66.6 0.1 collective-permute-done.18
  66.7 3.2 %collective-permute-done.20 = bf16[4,6144]{1,0:T(4,128)(2,1)S(1)} collective-permute-done((bf16[4,6144]{1,0:T(4,128)(2,1)S(1)}, bf16[4,6144]{1,0:T(4,128)(2,1)S(1)}, u32[]{:S(2)}, u32[]{:S(2)}) %collective-permute-start.20) | collective-permute-done | bytes 49184 | tf_op jit(solution)/shard_map/ppermute | solution.py:20
  69.9 2.0 %collective-permute-done.19 = bf16[4,6144]{1,0:T(4,128)(2,1)S(1)} collective-permute-done((bf16[4,6144]{1,0:T(4,128)(2,1)S(1)}, bf16[4,6144]{1,0:T(4,128)(2,1)S(1)}, u32[]{:S(2)}, u32[]{:S(2)}) %collective-permute-start.19) | collective-permute-done | bytes 49184 | tf_op jit(solution)/shard_map/ppermute | solution.py:20
  71.9 0.7 fusion.3
  (5 shorter events, 0.2 us)
Async XLA Ops:
  2.4 12.2 %copy-start.1 = (bf16[4,6144]{1,0:T(4,128)(2,1)S(1)}, bf16[4,6144]{1,0:T(4,128)(2,1)}, u32[]{:S(2)}) copy-start(bf16[4,6144]{1,0:T(4,128)(2,1)} %param.6) | copy-start | bytes 147460
  2.4 12.2 %collective-permute-start.2 = (bf16[4,6272]{1,0:T(4,128)(2,1)S(1)}, bf16[4,6272]{1,0:T(4,128)(2,1)S(1)}, u32[]{:S(2)}, u32[]{:S(2)}) collective-permute-start(bf16[4,6272]{1,0:T(4,128)(2,1)S(1)} %pad_maximum_fusion.2.refs_2_), channel_id=1, source_target_pairs={{0,12},{1,13},{2,14},{3,15},{4,8},{5,9},{6,10},{7,11},{8,4},{9,5},... | collective-permute-start | bytes 150536 | tf_op jit(solution)/shard_map/ppermute | solution.py:20
  7.5 7.1 %collective-permute-start.1 = (bf16[4,6272]{1,0:T(4,128)(2,1)S(1)}, bf16[4,6272]{1,0:T(4,128)(2,1)S(1)}, u32[]{:S(2)}, u32[]{:S(2)}) collective-permute-start(bf16[4,6272]{1,0:T(4,128)(2,1)S(1)} %pad_maximum_fusion.2.refs_2_), channel_id=1, source_target_pairs={{0,8},{1,9},{2,10},{3,11},{4,12},{5,13},{6,14},{7,15},{8,0},{9,1},... | collective-permute-start | bytes 150536 | tf_op jit(solution)/shard_map/ppermute | solution.py:20
  7.5 7.1 %collective-permute-start = (bf16[4,6272]{1,0:T(4,128)(2,1)S(1)}, bf16[4,6272]{1,0:T(4,128)(2,1)S(1)}, u32[]{:S(2)}, u32[]{:S(2)}) collective-permute-start(bf16[4,6272]{1,0:T(4,128)(2,1)S(1)} %pad_maximum_fusion.2.refs_2_), channel_id=1, source_target_pairs={{0,4},{1,5},{2,6},{3,7},{4,0},{5,1},{6,2},{7,3},{8,12},{9,13},{10,... | collective-permute-start | bytes 150536 | tf_op jit(solution)/shard_map/ppermute | solution.py:20
  14.8 10.0 %collective-permute-start.3 = (bf16[16,6272]{1,0:T(8,128)(2,1)S(1)}, bf16[16,6272]{1,0:T(8,128)(2,1)S(1)}, u32[]{:S(2)}, u32[]{:S(2)}) collective-permute-start(bf16[16,6272]{1,0:T(8,128)(2,1)S(1)} %pad_maximum_fusion.1.refs_2_.refs_4_), channel_id=1, source_target_pairs={{0,18},{1,19},{2,16},{3,17},{4,22},{5,23},{6,20},{7,21},{8,26},{9,... | collective-permute-start | bytes 602120 | tf_op jit(solution)/shard_map/ppermute | solution.py:20
  17.4 8.9 %collective-permute-start.5 = (bf16[16,6272]{1,0:T(8,128)(2,1)S(1)}, bf16[16,6272]{1,0:T(8,128)(2,1)S(1)}, u32[]{:S(2)}, u32[]{:S(2)}) collective-permute-start(bf16[16,6272]{1,0:T(8,128)(2,1)S(1)} %pad_maximum_fusion.1.refs_2_.refs_4_), channel_id=1, source_target_pairs={{0,16},{1,17},{2,18},{3,19},{4,20},{5,21},{6,22},{7,23},{8,24},{9,... | collective-permute-start | bytes 602120 | tf_op jit(solution)/shard_map/ppermute | solution.py:20
  18.0 8.3 %collective-permute-start.4 = (bf16[16,6272]{1,0:T(8,128)(2,1)S(1)}, bf16[16,6272]{1,0:T(8,128)(2,1)S(1)}, u32[]{:S(2)}, u32[]{:S(2)}) collective-permute-start(bf16[16,6272]{1,0:T(8,128)(2,1)S(1)} %pad_maximum_fusion.1.refs_2_.refs_4_), channel_id=1, source_target_pairs={{0,2},{1,3},{2,0},{3,1},{4,6},{5,7},{6,4},{7,5},{8,10},{9,11},{10,... | collective-permute-start | bytes 602120 | tf_op jit(solution)/shard_map/ppermute | solution.py:20
  18.3 8.5 %collective-permute-start.6 = (bf16[16,6272]{1,0:T(8,128)(2,1)S(1)}, bf16[16,6272]{1,0:T(8,128)(2,1)S(1)}, u32[]{:S(2)}, u32[]{:S(2)}) collective-permute-start(bf16[16,6272]{1,0:T(8,128)(2,1)S(1)} %pad_maximum_fusion.1.refs_2_.refs_4_), channel_id=1, source_target_pairs={{0,1},{1,0},{2,3},{3,2},{4,5},{5,4},{6,7},{7,6},{8,9},{9,8},{10,11... | collective-permute-start | bytes 602120 | tf_op jit(solution)/shard_map/ppermute | solution.py:20
  24.8 3.6 %copy-start = (f32[8,128]{1,0:T(8,128)}, f32[8,128]{1,0:T(8,128)S(1)}, u32[]{:S(2)}) copy-start(f32[8,128]{1,0:T(8,128)S(1)} %get-tuple-element.25.refs_3_) | copy-start | bytes 12292
  26.3 1.4 %collective-permute-start.8 = (bf16[16,6272]{1,0:T(8,128)(2,1)S(1)}, bf16[16,6272]{1,0:T(8,128)(2,1)S(1)}, u32[]{:S(2)}, u32[]{:S(2)}) collective-permute-start(bf16[16,6272]{1,0:T(8,128)(2,1)S(1)} %collective-permute-done.5.refs_6_), channel_id=1, source_target_pairs={{0,1},{1,0},{2,3},{3,2},{4,5},{5,4},{6,7},{7,6},{8,9},{9,8},{10,11... | collective-permute-start | bytes 602120 | tf_op jit(solution)/shard_map/ppermute | solution.py:20
  26.3 1.7 %collective-permute-start.7 = (bf16[16,6272]{1,0:T(8,128)(2,1)S(1)}, bf16[16,6272]{1,0:T(8,128)(2,1)S(1)}, u32[]{:S(2)}, u32[]{:S(2)}) collective-permute-start(bf16[16,6272]{1,0:T(8,128)(2,1)S(1)} %collective-permute-done.4.refs_5_), channel_id=1, source_target_pairs={{0,1},{1,0},{2,3},{3,2},{4,5},{5,4},{6,7},{7,6},{8,9},{9,8},{10,11... | collective-permute-start | bytes 602120 | tf_op jit(solution)/shard_map/ppermute | solution.py:20
  26.8 1.5 %collective-permute-start.9 = (bf16[16,6272]{1,0:T(8,128)(2,1)S(1)}, bf16[16,6272]{1,0:T(8,128)(2,1)S(1)}, u32[]{:S(2)}, u32[]{:S(2)}) collective-permute-start(bf16[16,6272]{1,0:T(8,128)(2,1)S(1)} %collective-permute-done.3.refs_7_), channel_id=1, source_target_pairs={{0,1},{1,0},{2,3},{3,2},{4,5},{5,4},{6,7},{7,6},{8,9},{9,8},{10,11... | collective-permute-start | bytes 602120 | tf_op jit(solution)/shard_map/ppermute | solution.py:20
  48.0 1.8 %collective-permute-start.10 = (bf16[64,3072]{1,0:T(8,128)(2,1)S(1)}, bf16[64,3072]{1,0:T(8,128)(2,1)S(1)}, u32[]{:S(2)}, u32[]{:S(2)}) collective-permute-start(bf16[64,3072]{1,0:T(8,128)(2,1)S(1)} %get-tuple-element.34), channel_id=1, source_target_pairs={{0,1},{1,0},{2,3},{3,2},{4,5},{5,4},{6,7},{7,6},{8,9},{9,8},{10,11... | collective-permute-start | bytes 1179656 | tf_op jit(solution)/shard_map/ppermute | solution.py:20
  48.3 5.2 %collective-permute-start.14 = (bf16[64,3072]{1,0:T(8,128)(2,1)S(1)}, bf16[64,3072]{1,0:T(8,128)(2,1)S(1)}, u32[]{:S(2)}, u32[]{:S(2)}) collective-permute-start(bf16[64,3072]{1,0:T(8,128)(2,1)S(1)} %get-tuple-element.36), channel_id=1, source_target_pairs={{0,1},{1,0},{2,3},{3,2},{4,5},{5,4},{6,7},{7,6},{8,9},{9,8},{10,11... | collective-permute-start | bytes 1179656 | tf_op jit(solution)/shard_map/ppermute | solution.py:20
  49.9 6.9 %collective-permute-start.11 = (bf16[16,3072]{1,0:T(8,128)(2,1)S(1)}, bf16[16,3072]{1,0:T(8,128)(2,1)S(1)}, u32[]{:S(2)}, u32[]{:S(2)}) collective-permute-start(bf16[16,3072]{1,0:T(8,128)(2,1)S(1)} %get-tuple-element.44), channel_id=1, source_target_pairs={{0,2},{1,3},{2,0},{3,1},{4,6},{5,7},{6,4},{7,5},{8,10},{9,11},{10,... | collective-permute-start | bytes 294920 | tf_op jit(solution)/shard_map/ppermute | solution.py:20
  51.1 7.1 %collective-permute-start.13 = (bf16[16,3072]{1,0:T(8,128)(2,1)S(1)}, bf16[16,3072]{1,0:T(8,128)(2,1)S(1)}, u32[]{:S(2)}, u32[]{:S(2)}) collective-permute-start(bf16[16,3072]{1,0:T(8,128)(2,1)S(1)} %get-tuple-element.45), channel_id=1, source_target_pairs={{0,18},{1,19},{2,16},{3,17},{4,22},{5,23},{6,20},{7,21},{8,26},{9,... | collective-permute-start | bytes 294920 | tf_op jit(solution)/shard_map/ppermute | solution.py:20
  52.9 6.3 %collective-permute-start.12 = (bf16[16,3072]{1,0:T(8,128)(2,1)S(1)}, bf16[16,3072]{1,0:T(8,128)(2,1)S(1)}, u32[]{:S(2)}, u32[]{:S(2)}) collective-permute-start(bf16[16,3072]{1,0:T(8,128)(2,1)S(1)} %get-tuple-element.46), channel_id=1, source_target_pairs={{0,16},{1,17},{2,18},{3,19},{4,20},{5,21},{6,22},{7,23},{8,24},{9,... | collective-permute-start | bytes 294920 | tf_op jit(solution)/shard_map/ppermute | solution.py:20
  53.6 7.0 %collective-permute-start.15 = (bf16[16,3072]{1,0:T(8,128)(2,1)S(1)}, bf16[16,3072]{1,0:T(8,128)(2,1)S(1)}, u32[]{:S(2)}, u32[]{:S(2)}) collective-permute-start(bf16[16,3072]{1,0:T(8,128)(2,1)S(1)} %get-tuple-element.41), channel_id=1, source_target_pairs={{0,2},{1,3},{2,0},{3,1},{4,6},{5,7},{6,4},{7,5},{8,10},{9,11},{10,... | collective-permute-start | bytes 294920 | tf_op jit(solution)/shard_map/ppermute | solution.py:20
  54.8 7.0 %collective-permute-start.17 = (bf16[16,3072]{1,0:T(8,128)(2,1)S(1)}, bf16[16,3072]{1,0:T(8,128)(2,1)S(1)}, u32[]{:S(2)}, u32[]{:S(2)}) collective-permute-start(bf16[16,3072]{1,0:T(8,128)(2,1)S(1)} %get-tuple-element.42), channel_id=1, source_target_pairs={{0,18},{1,19},{2,16},{3,17},{4,22},{5,23},{6,20},{7,21},{8,26},{9,... | collective-permute-start | bytes 294920 | tf_op jit(solution)/shard_map/ppermute | solution.py:20
  56.8 5.7 %collective-permute-start.16 = (bf16[16,3072]{1,0:T(8,128)(2,1)S(1)}, bf16[16,3072]{1,0:T(8,128)(2,1)S(1)}, u32[]{:S(2)}, u32[]{:S(2)}) collective-permute-start(bf16[16,3072]{1,0:T(8,128)(2,1)S(1)} %get-tuple-element.43), channel_id=1, source_target_pairs={{0,16},{1,17},{2,18},{3,19},{4,20},{5,21},{6,22},{7,23},{8,24},{9,... | collective-permute-start | bytes 294920 | tf_op jit(solution)/shard_map/ppermute | solution.py:20
  62.6 4.2 %collective-permute-start.18 = (bf16[4,6144]{1,0:T(4,128)(2,1)S(1)}, bf16[4,6144]{1,0:T(4,128)(2,1)S(1)}, u32[]{:S(2)}, u32[]{:S(2)}) collective-permute-start(bf16[4,6144]{1,0:T(4,128)(2,1)S(1)} %get-tuple-element.47), channel_id=1, source_target_pairs={{0,4},{1,5},{2,6},{3,7},{4,0},{5,1},{6,2},{7,3},{8,12},{9,13},{10,... | collective-permute-start | bytes 147464 | tf_op jit(solution)/shard_map/ppermute | solution.py:20
  64.0 5.9 %collective-permute-start.20 = (bf16[4,6144]{1,0:T(4,128)(2,1)S(1)}, bf16[4,6144]{1,0:T(4,128)(2,1)S(1)}, u32[]{:S(2)}, u32[]{:S(2)}) collective-permute-start(bf16[4,6144]{1,0:T(4,128)(2,1)S(1)} %get-tuple-element.48), channel_id=1, source_target_pairs={{0,12},{1,13},{2,14},{3,15},{4,8},{5,9},{6,10},{7,11},{8,4},{9,5},... | collective-permute-start | bytes 147464 | tf_op jit(solution)/shard_map/ppermute | solution.py:20
  66.4 5.5 %collective-permute-start.19 = (bf16[4,6144]{1,0:T(4,128)(2,1)S(1)}, bf16[4,6144]{1,0:T(4,128)(2,1)S(1)}, u32[]{:S(2)}, u32[]{:S(2)}) collective-permute-start(bf16[4,6144]{1,0:T(4,128)(2,1)S(1)} %get-tuple-element.49), channel_id=1, source_target_pairs={{0,8},{1,9},{2,10},{3,11},{4,12},{5,13},{6,14},{7,15},{8,0},{9,1},... | collective-permute-start | bytes 147464 | tf_op jit(solution)/shard_map/ppermute | solution.py:20

commit v2 on v1

--- a/solution.py
+++ b/solution.py
@@ -11,7 +11,7 @@
 VMEM = pl.BlockSpec(memory_space=pltpu.VMEM)
 HBM = pl.BlockSpec(memory_space=pltpu.HBM)
 MIB = 1 << 20
-RING = 6
+SIDES = 2
 
 
 def exchange(x, ke, kt):
@@ -81,9 +81,8 @@
 
 
 def columns(count, step, body):
-    @pl.loop(0, count // step)
-    def _(i):
-        body(pl.ds(pl.multiple_of(i * step, step), step))
+    for i in range(0, count, step):
+        body(slice(i, i + step))
 
 
 def dot(a, b):
@@ -100,20 +99,49 @@
     fb = min(256, f)
     rows = own * (nt // 4)
 
-    experts = lax.broadcasted_iota(jnp.int32, (1, LANES), 1)
-    gates = sum(
-        jnp.where(expert_ids[:, i : i + 1] == experts, gate_weights[:, i : i + 1], jnp.bfloat16(0))
-        for i in range(expert_ids.shape[1])
-    )
-    packed = jnp.concatenate([gates, tokens], axis=1)
+    top = expert_ids.shape[1]
+
+    def pack(gates_hbm, ids_hbm, tokens_hbm, out_ref, gates_ref, ids_ref, sems):
+        copies = [
+            pltpu.make_async_copy(gates_hbm, gates_ref, sems.at[0]),
+            pltpu.make_async_copy(ids_hbm, ids_ref, sems.at[1]),
+            pltpu.make_async_copy(tokens_hbm, out_ref.at[:, pl.ds(LANES, d)], sems.at[2]),
+        ]
+        for copy in copies:
+            copy.start()
+        row = lax.broadcasted_iota(jnp.int32, (own, own), 0)
+        diagonal = row == lax.broadcasted_iota(jnp.int32, (own, own), 1)
+        lane = lax.broadcasted_iota(jnp.int32, (own, LANES), 1)
+        meta = jnp.zeros((own, LANES), jnp.float32)
+        for n, ref in enumerate((gates_ref, ids_ref)):
+            copies[n].wait()
+            for i in range(top):
+                line = ref[i : i + 1, :].astype(jnp.float32)
+                col = jnp.sum(jnp.where(diagonal, line, 0.0), axis=1, keepdims=True)
+                meta = jnp.where(lane == n * top + i, col, meta)
+        out_ref[:, :LANES] = meta.astype(jnp.bfloat16)
+        copies[2].wait()
+
+    packed = pl.pallas_call(
+        pack,
+        in_specs=[HBM] * 3,
+        out_specs=VMEM,
+        out_shape=pltpu.VMEM((own, LANES + d), jnp.bfloat16),
+        scratch_shapes=[
+            pltpu.VMEM((top, own), gate_weights.dtype),
+            pltpu.VMEM((top, own), expert_ids.dtype),
+            pltpu.SemaphoreType.DMA((3,)),
+        ],
+        compiler_params=pltpu.CompilerParams(vmem_limit_bytes=MIB),
+    )(*[pltpu.with_memory_space_constraint(x, pltpu.HBM) for x in (gate_weights.T, expert_ids.T, tokens)])
 
     def load_only(loads, *deps):
         units, token, _ = stage(None, weights, loads, deps, [], [], [], 0, 2 * MIB)
         return units, token
 
     last = e_count - 1
-    resident = [(k, e, h, half) for e in range(last) for k in (0, 1) for h in (0, 1)]
-    resident += [(0, last, 0, half), (1, last, 0, half)]
+    resident = [(k, last, 0, half) for k in (0, 1)]
+    resident += [(k, e, h, half) for e in range(last) for k in (0, 1) for h in (0, 1)]
     cut = len(resident) // 2
     far = [exchange(packed, *k) for k in far_offsets()]
     units, token = load_only(resident[:cut], packed)
@@ -126,10 +154,10 @@
     pieces = pieces + [exchange(p, 0, 1) for p in pieces]
 
     chunk = 1024
-    n_k, n_d = half // chunk, d // chunk
-    stream = [(k, j) for j in range(n_k) for k in (0, 1)]
-    stream += [(2 + e, j) for j in range(n_d) for e in range(e_count)]
-    slots = RING
+    n_d = d // chunk
+    down = [(e, j) for j in range(n_d) for e in range(e_count)]
+    per_unit = half // chunk
+    spares = len(down) // per_unit if f == chunk and len(down) <= 4 * per_unit else 0
 
     def kernel(*refs):
         refs = list(refs)
@@ -137,107 +165,95 @@
         del refs[:4]
         xrefs = [refs.pop(0) for _ in pieces]
         held = {spot[:3]: refs.pop(0) for spot in resident}
-        sends = [refs.pop(0) for _ in range(2)]
-        keeps = [refs.pop(0) for _ in range(2)]
-        xs, gate_ref, g_ref, u_ref, h_ref, ring, sems = refs
+        sends = [refs.pop(0) for _ in range(SIDES)]
+        keeps = [refs.pop(0) for _ in range(SIDES)]
+        spare = [refs.pop(0) for _ in range(spares)]
+        xs, gate_ref, h_ref, tail, landing, sems = refs
 
         def slot(i):
-            kind, j = stream[i]
-            view = ring.at[i % slots]
-            return view.at[:chunk, :f] if kind < 2 else view.at[:f, :chunk]
-
-        def copy(i):
-            kind, j = stream[i]
-            if kind < 2:
-                src = (wg, wu)[kind].at[last, pl.ds(half + j * chunk, chunk), :]
-            else:
-                src = wd.at[kind - 2, :, pl.ds(j * chunk, chunk)]
-            return pltpu.make_async_copy(src, slot(i), sems.at[i % slots])
-
-        for i in range(slots):
-            copy(i).start()
-
+            return spare[i // per_unit].at[pl.ds(i % per_unit * chunk, chunk), :] if spares else landing.at[i]
+
+        tails = [
+            pltpu.make_async_copy(w.at[last, pl.ds(half, half), :], tail.at[k], sems.at[k])
+            for k, w in enumerate((wg, wu))
+        ]
+        downs = [
+            pltpu.make_async_copy(wd.at[e, :, pl.ds(j * chunk, chunk)], slot(i), sems.at[2 + i])
+            for i, (e, j) in enumerate(down)
+        ]
+        for copy in tails:
+            copy.start()
         me = lax.axis_index("expert")
         for i, ref in enumerate(xrefs):
             r = slice(i * rows, (i + 1) * rows)
             xs[r, :] = ref[:, LANES:]
             meta = ref[:, :LANES].astype(jnp.float32)
-            lane = lax.broadcasted_iota(jnp.int32, meta.shape, 1)
             for e in range(e_count):
-                col = jnp.sum(jnp.where(lane == me * e_count + e, meta, 0.0), axis=1, keepdims=True)
+                expert = (me * e_count + e).astype(jnp.float32)
+                col = sum(
+                    jnp.where(meta[:, top + i : top + i + 1] == expert, meta[:, i : i + 1], 0.0)
+                    for i in range(top)
+                )
                 gate_ref[e, r, :] = jnp.broadcast_to(col, meta.shape)
 
-        def hide(e, c, g, u):
-            h_ref[e, :, c] = (g / (1.0 + jnp.exp(-g)) * u).astype(jnp.bfloat16)
-
-        def begin(c):
-            g_ref[:, c] = dot(xs[:, :half], held[0, last, 0][:, c])
-            u_ref[:, c] = dot(xs[:, :half], held[1, last, 0][:, c])
-
-        columns(f, fb, begin)
-        for j in range(n_k):
-            k = slice(half + j * chunk, half + (j + 1) * chunk)
-            sg, su = slot(2 * j), slot(2 * j + 1)
-            copy(2 * j).wait()
-            copy(2 * j + 1).wait()
-
-            def add(c):
-                g = g_ref[:, c] + dot(xs[:, k], sg[:, c])
-                u = u_ref[:, c] + dot(xs[:, k], su[:, c])
-                if j < n_k - 1:
-                    g_ref[:, c] = g
-                    u_ref[:, c] = u
-                else:
-                    hide(last, c, g, u)
-
-            columns(f, fb, add)
-            for i in (2 * j, 2 * j + 1):
-                if i + slots < len(stream):
-                    copy(i + slots).start()
-        for e in range(last):
-
-            def whole(c):
-                g = dot(xs[:, :half], held[0, e, 0][:, c]) + dot(xs[:, half:], held[0, e, 1][:, c])
-                u = dot(xs[:, :half], held[1, e, 0][:, c]) + dot(xs[:, half:], held[1, e, 1][:, c])
-                hide(e, c, g, u)
-
-            columns(f, fb, whole)
+        for e in range(e_count):
+            def part(k, h):
+                return tail.at[k] if e == last and h else held[k, e, h]
+
+            if e == last:
+                for copy in tails:
+                    copy.wait()
+
+            def hide(c):
+                g = dot(xs[:, :half], part(0, 0)[:, c]) + dot(xs[:, half:], part(0, 1)[:, c])
+                u = dot(xs[:, :half], part(1, 0)[:, c]) + dot(xs[:, half:], part(1, 1)[:, c])
+                h_ref[e, :, c] = (g / (1.0 + jnp.exp(-g)) * u).astype(jnp.bfloat16)
+
+            if e < last:
+
+                @pl.when(me >= 0)
+                def _():
+                    columns(f, fb, hide)
+            else:
+                columns(f, fb, hide)
+
+            if e == 0:
+                for copy in downs:
+                    copy.start()
         for j in range(n_d):
-            at = [2 * n_k + j * e_count + e for e in range(e_count)]
+            at = range(j * e_count, (j + 1) * e_count)
             views = [slot(i) for i in at]
             for i in at:
-                copy(i).wait()
-            side, start = divmod(j * chunk, half)
+                downs[i].wait()
+            side, start = divmod(j * chunk, d // SIDES)
 
             def out(c):
                 s = sum(dot(h_ref[e], views[e][:, c]) * gate_ref[e, :, 0:1] for e in range(e_count))
-                to = pl.ds(pl.multiple_of(c.start + start, 256), 256)
+                to = slice(c.start + start, c.stop + start)
                 keeps[side][:, to] = s[: total // 2]
                 sends[side][:, to] = s[total // 2 :].astype(jnp.bfloat16)
 
             columns(chunk, 256, out)
-            for i in at:
-                if i + slots < len(stream):
-                    copy(i + slots).start()
-
-    side_len = max(chunk, f)
-    scratch = 2 * total * d + 4 * e_count * total * LANES + 8 * total * f + 2 * e_count * total * f
-    scratch += 2 * slots * side_len * side_len
+
+    landing = (1, 16, LANES) if spares else (len(down), f, chunk)
+    scratch = 2048 * total + 2 * total * d + 4 * e_count * total * LANES + 2 * e_count * total * f
+    scratch += 4 * half * f + 2 * landing[0] * landing[1] * landing[2]
     ins = pieces + units
     results = pl.pallas_call(
         kernel,
         in_specs=[HBM] * 3 + [pl.BlockSpec(memory_space=pl.ANY)] + [VMEM] * len(ins),
-        out_specs=[VMEM] * 4,
-        out_shape=[pltpu.VMEM((total // 2, half), jnp.bfloat16)] * 2
-        + [pltpu.VMEM((total // 2, half), jnp.float32)] * 2,
+        out_specs=[VMEM] * (2 * SIDES + spares),
+        out_shape=[pltpu.VMEM((total // 2, d // SIDES), jnp.bfloat16)] * SIDES
+        + [pltpu.VMEM((total // 2, d // SIDES), jnp.float32)] * SIDES
+        + [pltpu.VMEM((half, f), jnp.bfloat16)] * spares,
+        input_output_aliases={4 + len(pieces) + 2 + i: 2 * SIDES + i for i in range(spares)},
         scratch_shapes=[
             pltpu.VMEM((total, d), jnp.bfloat16),
             pltpu.VMEM((e_count, total, LANES), jnp.float32),
-            pltpu.VMEM((total, f), jnp.float32),
-            pltpu.VMEM((total, f), jnp.float32),
             pltpu.VMEM((e_count, total, f), jnp.bfloat16),
-            pltpu.VMEM((slots, side_len, side_len), jnp.bfloat16),
-            pltpu.SemaphoreType.DMA((slots,)),
+            pltpu.VMEM((2, half, f), jnp.bfloat16),
+            pltpu.VMEM(landing, jnp.bfloat16),
+            pltpu.SemaphoreType.DMA((2 + len(down),)),
         ],
         compiler_params=pltpu.CompilerParams(vmem_limit_bytes=-(-scratch // MIB) * MIB),
         cost_estimate=pl.CostEstimate(
@@ -246,7 +262,7 @@
     )(*[pltpu.with_memory_space_constraint(w, pltpu.HBM) for w in weights], token, *[in_vmem(x) for x in ins])
 
     sums = []
-    for send, keep in zip(results[:2], results[2:]):
+    for send, keep in zip(results[:SIDES], results[SIDES : 2 * SIDES]):
         s = keep + exchange(send, 0, 1).astype(jnp.float32)
         got = [
             exchange(s[i * rows : (i + 1) * rows].astype(jnp.bfloat16), *k)

time: 72.8 us -> 65.4 us (0.90)
  Pallas kernels: 32.5 us -> 27.5 us
  local copies, waits for them, and re-layouts: 1.61 us -> 0.11 us
  other arithmetic: 1.99 us -> 1.09 us
    pallas_call x1, Pallas kernels: 19.6 us -> 13.8 us  [shards(): pl.pallas_call(kernel, in_specs=[HBM] * 3 + [pl.BlockSpec(memory_space=pl...]
    pallas_call x0 -> x1, Pallas kernels: none -> 0.86 us  [shards(): pl.pallas_call(pack, in_specs=[HBM] * 3, out_specs=VMEM, out_shape=pltpu....]
    concatenate x1 -> x0, other arithmetic: 0.82 us -> none  [shards(): packed = jnp.concatenate([gates, tokens], axis=1)]
    eq x1 -> x0, local copies, waits for them, and re-layouts: 0.76 us -> none  [shards(): expert_ids[:, i:i + 1] == experts]
    broadcast_in_dim x1 -> x0, local copies, waits for them, and re-layouts: 0.73 us -> none  [shards(): jnp.where(expert_ids[:, i:i + 1] == experts, gate_weights[:, i:i + 1], jn...]
  transfers between devices with their start and end apart: 21 -> 21, of which waited for: 13 -> 13; matrix products, arithmetic and copies ran while one was open for 0% -> 0% of each run, Pallas kernels for 18% -> 20%
where the time goes in v2:
time: 65.4 us; the launch traced here: 65.2 us
  Pallas kernels  27.5 us (42%)
  starting transfers between devices  22.5 us (34%)
  waiting for transfers between devices  13.8 us (21%)
  other arithmetic  1.09 us (2%)
    ppermute x21, starting transfers between devices, exchange(): return lax.ppermute(x, BOTH, pairs)  22.5 us
    pallas_call x1, Pallas kernels, shards(): pl.pallas_call(kernel, in_specs=[HBM] * 3 + [pl.BlockSpec(memory_space=pl...  13.8 us
    ppermute x21, waiting for transfers between devices, exchange(): return lax.ppermute(x, BOTH, pairs)  13.8 us
    pallas_call x2, Pallas kernels, stage(): pl.pallas_call(kernel, in_specs=[HBM] * len(used) + [pl.BlockSpec(memory_...  12.8 us
  transfers between devices with their start and end apart: 21, of which 13 were waited for; matrix products, arithmetic and copies ran while one was open for 0% of the time, Pallas kernels for 20%

profile of v2, /device:TPU:0, one launch (start us, length us, event | category | flops | bytes accessed | tf_op | source)
XLA Modules:
  0.0 65.2 jit_solution(2148538368815828161)
XLA Ops:
  0.0 0.9 %shard_map.64.refs_2_ = bf16[4,6272]{1,0:T(4,128)(2,1)S(1)} custom-call(bf16[2,4]{1,0:T(2,128)(2,1)} %bitcast.3, s32[2,4]{1,0:T(2,128)} %bitcast.2, bf16[4,6144]{1,0:T(4,128)(2,1)} %tokens_hbm.1), custom_call_target="tpu_custom_call" | custom-call | tf_op jit(solution)/shard_map/pallas_call | solution.py:125
  0.9 5.1 %collective-permute-start.2 = (bf16[4,6272]{1,0:T(4,128)(2,1)S(1)}, bf16[4,6272]{1,0:T(4,128)(2,1)S(1)}, u32[]{:S(2)}, u32[]{:S(2)}) collective-permute-start(bf16[4,6272]{1,0:T(4,128)(2,1)S(1)} %shard_map.64.refs_2_), channel_id=1, source_target_pairs={{0,12},{1,13},{2,14},{3,15},{4,8},{5,9},{6,10},{7,11},{8,4},{9,5},... | collective-permute-start | bytes 150536 | tf_op jit(solution)/shard_map/ppermute | solution.py:20
  6.0 0.0 collective-permute-start.1
  6.0 0.6 collective-permute-start
  6.6 6.4 %shard_map.65 = (bf16[3072,1024]{1,0:T(8,128)(2,1)S(1)}, bf16[3072,1024]{1,0:T(8,128)(2,1)S(1)}, bf16[3072,1024]{1,0:T(8,128)(2,1)S(1)}, f32[8,128]{1,0:T(8,128)S(1)}) custom-call(bf16[2,6144,1024]{2,1,0:T(8,128)(2,1)} %refs_0_.5, bf16[2,6144,1024]{2,1,0:T(8,128)(2,1)} %refs_1_.5, bf16[4,6272]{1,0:T(4,128)(2,1)S(1)} %shard_map.64.refs_2_), custom_call_target="tpu_custom_call" | custom-call | bytes 18874368 | tf_op jit(solution)/shard_map/pallas_call | solution.py:69
  13.1 0.0 collective-permute-done.2
  13.1 0.0 collective-permute-done.1
  13.1 0.0 collective-permute-done
  13.1 0.1 pad_maximum_fusion.1.refs_2_.refs_4_
  13.2 2.7 %collective-permute-start.3 = (bf16[16,6272]{1,0:T(8,128)(2,1)S(1)}, bf16[16,6272]{1,0:T(8,128)(2,1)S(1)}, u32[]{:S(2)}, u32[]{:S(2)}) collective-permute-start(bf16[16,6272]{1,0:T(8,128)(2,1)S(1)} %pad_maximum_fusion.1.refs_2_.refs_4_), channel_id=1, source_target_pairs={{0,18},{1,19},{2,16},{3,17},{4,22},{5,23},{6,20},{7,21},{8,26},{9,... | collective-permute-start | bytes 602120 | tf_op jit(solution)/shard_map/ppermute | solution.py:20
  15.9 0.5 collective-permute-start.5
  16.4 0.4 collective-permute-start.4
  16.8 0.0 collective-permute-start.6
  16.8 6.4 %shard_map.66 = (bf16[3072,1024]{1,0:T(8,128)(2,1)S(1)}, bf16[3072,1024]{1,0:T(8,128)(2,1)S(1)}, bf16[3072,1024]{1,0:T(8,128)(2,1)S(1)}, f32[8,128]{1,0:T(8,128)S(1)}) custom-call(bf16[2,6144,1024]{2,1,0:T(8,128)(2,1)} %refs_0_.5, bf16[2,6144,1024]{2,1,0:T(8,128)(2,1)} %refs_1_.5, bf16[16,6272]{1,0:T(8,128)(2,1)S(1)} %pad_maximum_fusion.1.refs_2_.refs_4_, ...), custom_call_target="tpu_custom_call" | custom-call | bytes 18874368 | tf_op jit(solution)/shard_map/pallas_call | solution.py:69
  23.2 0.0 copy-start
  23.2 0.0 collective-permute-done.3.refs_7_
  23.2 1.5 %collective-permute-done.5.refs_6_ = bf16[16,6272]{1,0:T(8,128)(2,1)S(1)} collective-permute-done((bf16[16,6272]{1,0:T(8,128)(2,1)S(1)}, bf16[16,6272]{1,0:T(8,128)(2,1)S(1)}, u32[]{:S(2)}, u32[]{:S(2)}) %collective-permute-start.5) | collective-permute-done | bytes 200736 | tf_op jit(solution)/shard_map/ppermute | solution.py:20
  24.7 0.0 collective-permute-start.8
  24.8 0.0 collective-permute-done.4.refs_5_
  24.8 0.5 collective-permute-start.7
  25.3 0.0 collective-permute-start.9
  25.3 0.0 collective-permute-done.6.refs_8_
  25.3 0.9 %collective-permute-done.8.refs_10_ = bf16[16,6272]{1,0:T(8,128)(2,1)S(1)} collective-permute-done((bf16[16,6272]{1,0:T(8,128)(2,1)S(1)}, bf16[16,6272]{1,0:T(8,128)(2,1)S(1)}, u32[]{:S(2)}, u32[]{:S(2)}) %collective-permute-start.8) | collective-permute-done | bytes 200736 | tf_op jit(solution)/shard_map/ppermute | solution.py:20
  26.2 0.3 collective-permute-done.7.refs_9_
  26.5 0.3 collective-permute-done.9.refs_11_
  26.8 0.0 copy-done
  26.8 13.8 %shard_map.67 = (bf16[64,3072]{1,0:T(8,128)(2,1)S(1)}, bf16[64,3072]{1,0:T(8,128)(2,1)S(1)}, f32[64,3072]{1,0:T(8,128)S(1)}, f32[64,3072]{1,0:T(8,128)S(1)}, bf1...) custom-call(bf16[2,6144,1024]{2,1,0:T(8,128)(2,1)} %refs_0_.5, ...), custom_call_target="tpu_custom_call", output_to_operand_aliasing={{4}: (14, {}), {5}: (15, {}), {6}: (16, {}), {7}: (17, {})} | custom-call | flops 9663676416 | bytes 50331648 | tf_op jit(solution)/shard_map/pallas_call | solution.py:242
  40.6 0.3 collective-permute-start.10
  40.9 0.3 collective-permute-start.14
  41.2 1.2 %collective-permute-done.10 = bf16[64,3072]{1,0:T(8,128)(2,1)S(1)} collective-permute-done((bf16[64,3072]{1,0:T(8,128)(2,1)S(1)}, bf16[64,3072]{1,0:T(8,128)(2,1)S(1)}, u32[]{:S(2)}, u32[]{:S(2)}) %collective-permute-start.10) | collective-permute-done | bytes 393248 | tf_op jit(solution)/shard_map/ppermute | solution.py:20
  42.4 0.1 fusion.5
  42.5 1.2 %collective-permute-start.11 = (bf16[16,3072]{1,0:T(8,128)(2,1)S(1)}, bf16[16,3072]{1,0:T(8,128)(2,1)S(1)}, u32[]{:S(2)}, u32[]{:S(2)}) collective-permute-start(bf16[16,3072]{1,0:T(8,128)(2,1)S(1)} %get-tuple-element.44), channel_id=1, source_target_pairs={{0,2},{1,3},{2,0},{3,1},{4,6},{5,7},{6,4},{7,5},{8,10},{9,11},{10,... | collective-permute-start | bytes 294920 | tf_op jit(solution)/shard_map/ppermute | solution.py:20
  43.7 1.8 %collective-permute-start.13 = (bf16[16,3072]{1,0:T(8,128)(2,1)S(1)}, bf16[16,3072]{1,0:T(8,128)(2,1)S(1)}, u32[]{:S(2)}, u32[]{:S(2)}) collective-permute-start(bf16[16,3072]{1,0:T(8,128)(2,1)S(1)} %get-tuple-element.45), channel_id=1, source_target_pairs={{0,18},{1,19},{2,16},{3,17},{4,22},{5,23},{6,20},{7,21},{8,26},{9,... | collective-permute-start | bytes 294920 | tf_op jit(solution)/shard_map/ppermute | solution.py:20
  45.6 0.5 collective-permute-start.12
  46.1 0.0 collective-permute-done.14
  46.1 0.1 fusion.4
  46.2 1.2 %collective-permute-start.15 = (bf16[16,3072]{1,0:T(8,128)(2,1)S(1)}, bf16[16,3072]{1,0:T(8,128)(2,1)S(1)}, u32[]{:S(2)}, u32[]{:S(2)}) collective-permute-start(bf16[16,3072]{1,0:T(8,128)(2,1)S(1)} %get-tuple-element.41), channel_id=1, source_target_pairs={{0,2},{1,3},{2,0},{3,1},{4,6},{5,7},{6,4},{7,5},{8,10},{9,11},{10,... | collective-permute-start | bytes 294920 | tf_op jit(solution)/shard_map/ppermute | solution.py:20
  47.4 1.8 %collective-permute-start.17 = (bf16[16,3072]{1,0:T(8,128)(2,1)S(1)}, bf16[16,3072]{1,0:T(8,128)(2,1)S(1)}, u32[]{:S(2)}, u32[]{:S(2)}) collective-permute-start(bf16[16,3072]{1,0:T(8,128)(2,1)S(1)} %get-tuple-element.42), channel_id=1, source_target_pairs={{0,18},{1,19},{2,16},{3,17},{4,22},{5,23},{6,20},{7,21},{8,26},{9,... | collective-permute-start | bytes 294920 | tf_op jit(solution)/shard_map/ppermute | solution.py:20
  49.2 0.1 collective-permute-done.11
  49.4 1.5 %collective-permute-start.16 = (bf16[16,3072]{1,0:T(8,128)(2,1)S(1)}, bf16[16,3072]{1,0:T(8,128)(2,1)S(1)}, u32[]{:S(2)}, u32[]{:S(2)}) collective-permute-start(bf16[16,3072]{1,0:T(8,128)(2,1)S(1)} %get-tuple-element.43), channel_id=1, source_target_pairs={{0,16},{1,17},{2,18},{3,19},{4,20},{5,21},{6,22},{7,23},{8,24},{9,... | collective-permute-start | bytes 294920 | tf_op jit(solution)/shard_map/ppermute | solution.py:20
  50.8 0.0 collective-permute-done.13
  50.8 1.0 %collective-permute-done.12 = bf16[16,3072]{1,0:T(8,128)(2,1)S(1)} collective-permute-done((bf16[16,3072]{1,0:T(8,128)(2,1)S(1)}, bf16[16,3072]{1,0:T(8,128)(2,1)S(1)}, u32[]{:S(2)}, u32[]{:S(2)}) %collective-permute-start.12) | collective-permute-done | bytes 98336 | tf_op jit(solution)/shard_map/ppermute | solution.py:20
  51.9 1.4 %collective-permute-done.15 = bf16[16,3072]{1,0:T(8,128)(2,1)S(1)} collective-permute-done((bf16[16,3072]{1,0:T(8,128)(2,1)S(1)}, bf16[16,3072]{1,0:T(8,128)(2,1)S(1)}, u32[]{:S(2)}, u32[]{:S(2)}) %collective-permute-start.15) | collective-permute-done | bytes 98336 | tf_op jit(solution)/shard_map/ppermute | solution.py:20
  53.2 1.3 %collective-permute-done.17 = bf16[16,3072]{1,0:T(8,128)(2,1)S(1)} collective-permute-done((bf16[16,3072]{1,0:T(8,128)(2,1)S(1)}, bf16[16,3072]{1,0:T(8,128)(2,1)S(1)}, u32[]{:S(2)}, u32[]{:S(2)}) %collective-permute-start.17) | collective-permute-done | bytes 98336 | tf_op jit(solution)/shard_map/ppermute | solution.py:20
  54.5 0.6 collective-permute-done.16
  55.2 0.1 fusion.8
  55.2 1.5 %collective-permute-start.18 = (bf16[4,6144]{1,0:T(4,128)(2,1)S(1)}, bf16[4,6144]{1,0:T(4,128)(2,1)S(1)}, u32[]{:S(2)}, u32[]{:S(2)}) collective-permute-start(bf16[4,6144]{1,0:T(4,128)(2,1)S(1)} %get-tuple-element.47), channel_id=1, source_target_pairs={{0,4},{1,5},{2,6},{3,7},{4,0},{5,1},{6,2},{7,3},{8,12},{9,13},{10,... | collective-permute-start | bytes 147464 | tf_op jit(solution)/shard_map/ppermute | solution.py:20
  56.7 2.4 %collective-permute-start.20 = (bf16[4,6144]{1,0:T(4,128)(2,1)S(1)}, bf16[4,6144]{1,0:T(4,128)(2,1)S(1)}, u32[]{:S(2)}, u32[]{:S(2)}) collective-permute-start(bf16[4,6144]{1,0:T(4,128)(2,1)S(1)} %get-tuple-element.48), channel_id=1, source_target_pairs={{0,12},{1,13},{2,14},{3,15},{4,8},{5,9},{6,10},{7,11},{8,4},{9,5},... | collective-permute-start | bytes 147464 | tf_op jit(solution)/shard_map/ppermute | solution.py:20
  59.0 0.3 collective-permute-start.19
  59.3 0.1 collective-permute-done.18
  59.4 3.2 %collective-permute-done.20 = bf16[4,6144]{1,0:T(4,128)(2,1)S(1)} collective-permute-done((bf16[4,6144]{1,0:T(4,128)(2,1)S(1)}, bf16[4,6144]{1,0:T(4,128)(2,1)S(1)}, u32[]{:S(2)}, u32[]{:S(2)}) %collective-permute-start.20) | collective-permute-done | bytes 49184 | tf_op jit(solution)/shard_map/ppermute | solution.py:20
  62.6 2.0 %collective-permute-done.19 = bf16[4,6144]{1,0:T(4,128)(2,1)S(1)} collective-permute-done((bf16[4,6144]{1,0:T(4,128)(2,1)S(1)}, bf16[4,6144]{1,0:T(4,128)(2,1)S(1)}, u32[]{:S(2)}, u32[]{:S(2)}) %collective-permute-start.19) | collective-permute-done | bytes 49184 | tf_op jit(solution)/shard_map/ppermute | solution.py:20
  64.6 0.7 %fusion.3 = bf16[4,6144]{1,0:T(4,128)(2,1)} fusion(f32[16,3072]{1,0:T(8,128)S(1)} %slice_add_fusion.1, f32[16,3072]{1,0:T(8,128)S(1)} %slice_add_fusion, bf16[4,6144]{1,0:T(4,128)(2,1)S(1)} %collective-permute-done.20, bf16[4,6144]{1,0:T(4,128)(2,1)S(1)} %collective-permute-done.19, bf16[4,6144]{1,0:T(4,128)(2,1)S(1)} %collective-permute-done.18), kind=kLoop, calls=%fused_computation.11 | loop fusion | flops 196608 | bytes 589824 | tf_op jit(solution)/shard_map/convert_element_type | solution.py:278
  (5 shorter events, 0.2 us)
Async XLA Ops:
  0.9 12.2 %collective-permute-start.2 = (bf16[4,6272]{1,0:T(4,128)(2,1)S(1)}, bf16[4,6272]{1,0:T(4,128)(2,1)S(1)}, u32[]{:S(2)}, u32[]{:S(2)}) collective-permute-start(bf16[4,6272]{1,0:T(4,128)(2,1)S(1)} %shard_map.64.refs_2_), channel_id=1, source_target_pairs={{0,12},{1,13},{2,14},{3,15},{4,8},{5,9},{6,10},{7,11},{8,4},{9,5},... | collective-permute-start | bytes 150536 | tf_op jit(solution)/shard_map/ppermute | solution.py:20
  6.0 7.1 %collective-permute-start.1 = (bf16[4,6272]{1,0:T(4,128)(2,1)S(1)}, bf16[4,6272]{1,0:T(4,128)(2,1)S(1)}, u32[]{:S(2)}, u32[]{:S(2)}) collective-permute-start(bf16[4,6272]{1,0:T(4,128)(2,1)S(1)} %shard_map.64.refs_2_), channel_id=1, source_target_pairs={{0,8},{1,9},{2,10},{3,11},{4,12},{5,13},{6,14},{7,15},{8,0},{9,1},... | collective-permute-start | bytes 150536 | tf_op jit(solution)/shard_map/ppermute | solution.py:20
  6.0 7.1 %collective-permute-start = (bf16[4,6272]{1,0:T(4,128)(2,1)S(1)}, bf16[4,6272]{1,0:T(4,128)(2,1)S(1)}, u32[]{:S(2)}, u32[]{:S(2)}) collective-permute-start(bf16[4,6272]{1,0:T(4,128)(2,1)S(1)} %shard_map.64.refs_2_), channel_id=1, source_target_pairs={{0,4},{1,5},{2,6},{3,7},{4,0},{5,1},{6,2},{7,3},{8,12},{9,13},{10,... | collective-permute-start | bytes 150536 | tf_op jit(solution)/shard_map/ppermute | solution.py:20
  13.2 10.0 %collective-permute-start.3 = (bf16[16,6272]{1,0:T(8,128)(2,1)S(1)}, bf16[16,6272]{1,0:T(8,128)(2,1)S(1)}, u32[]{:S(2)}, u32[]{:S(2)}) collective-permute-start(bf16[16,6272]{1,0:T(8,128)(2,1)S(1)} %pad_maximum_fusion.1.refs_2_.refs_4_), channel_id=1, source_target_pairs={{0,18},{1,19},{2,16},{3,17},{4,22},{5,23},{6,20},{7,21},{8,26},{9,... | collective-permute-start | bytes 602120 | tf_op jit(solution)/shard_map/ppermute | solution.py:20
  15.9 8.9 %collective-permute-start.5 = (bf16[16,6272]{1,0:T(8,128)(2,1)S(1)}, bf16[16,6272]{1,0:T(8,128)(2,1)S(1)}, u32[]{:S(2)}, u32[]{:S(2)}) collective-permute-start(bf16[16,6272]{1,0:T(8,128)(2,1)S(1)} %pad_maximum_fusion.1.refs_2_.refs_4_), channel_id=1, source_target_pairs={{0,16},{1,17},{2,18},{3,19},{4,20},{5,21},{6,22},{7,23},{8,24},{9,... | collective-permute-start | bytes 602120 | tf_op jit(solution)/shard_map/ppermute | solution.py:20
  16.4 8.3 %collective-permute-start.4 = (bf16[16,6272]{1,0:T(8,128)(2,1)S(1)}, bf16[16,6272]{1,0:T(8,128)(2,1)S(1)}, u32[]{:S(2)}, u32[]{:S(2)}) collective-permute-start(bf16[16,6272]{1,0:T(8,128)(2,1)S(1)} %pad_maximum_fusion.1.refs_2_.refs_4_), channel_id=1, source_target_pairs={{0,2},{1,3},{2,0},{3,1},{4,6},{5,7},{6,4},{7,5},{8,10},{9,11},{10,... | collective-permute-start | bytes 602120 | tf_op jit(solution)/shard_map/ppermute | solution.py:20
  16.8 8.5 %collective-permute-start.6 = (bf16[16,6272]{1,0:T(8,128)(2,1)S(1)}, bf16[16,6272]{1,0:T(8,128)(2,1)S(1)}, u32[]{:S(2)}, u32[]{:S(2)}) collective-permute-start(bf16[16,6272]{1,0:T(8,128)(2,1)S(1)} %pad_maximum_fusion.1.refs_2_.refs_4_), channel_id=1, source_target_pairs={{0,1},{1,0},{2,3},{3,2},{4,5},{5,4},{6,7},{7,6},{8,9},{9,8},{10,11... | collective-permute-start | bytes 602120 | tf_op jit(solution)/shard_map/ppermute | solution.py:20
  23.2 3.6 %copy-start = (f32[8,128]{1,0:T(8,128)}, f32[8,128]{1,0:T(8,128)S(1)}, u32[]{:S(2)}) copy-start(f32[8,128]{1,0:T(8,128)S(1)} %get-tuple-element.25.refs_3_) | copy-start | bytes 12292
  24.7 1.4 %collective-permute-start.8 = (bf16[16,6272]{1,0:T(8,128)(2,1)S(1)}, bf16[16,6272]{1,0:T(8,128)(2,1)S(1)}, u32[]{:S(2)}, u32[]{:S(2)}) collective-permute-start(bf16[16,6272]{1,0:T(8,128)(2,1)S(1)} %collective-permute-done.5.refs_6_), channel_id=1, source_target_pairs={{0,1},{1,0},{2,3},{3,2},{4,5},{5,4},{6,7},{7,6},{8,9},{9,8},{10,11... | collective-permute-start | bytes 602120 | tf_op jit(solution)/shard_map/ppermute | solution.py:20
  24.8 1.7 %collective-permute-start.7 = (bf16[16,6272]{1,0:T(8,128)(2,1)S(1)}, bf16[16,6272]{1,0:T(8,128)(2,1)S(1)}, u32[]{:S(2)}, u32[]{:S(2)}) collective-permute-start(bf16[16,6272]{1,0:T(8,128)(2,1)S(1)} %collective-permute-done.4.refs_5_), channel_id=1, source_target_pairs={{0,1},{1,0},{2,3},{3,2},{4,5},{5,4},{6,7},{7,6},{8,9},{9,8},{10,11... | collective-permute-start | bytes 602120 | tf_op jit(solution)/shard_map/ppermute | solution.py:20
  25.3 1.5 %collective-permute-start.9 = (bf16[16,6272]{1,0:T(8,128)(2,1)S(1)}, bf16[16,6272]{1,0:T(8,128)(2,1)S(1)}, u32[]{:S(2)}, u32[]{:S(2)}) collective-permute-start(bf16[16,6272]{1,0:T(8,128)(2,1)S(1)} %collective-permute-done.3.refs_7_), channel_id=1, source_target_pairs={{0,1},{1,0},{2,3},{3,2},{4,5},{5,4},{6,7},{7,6},{8,9},{9,8},{10,11... | collective-permute-start | bytes 602120 | tf_op jit(solution)/shard_map/ppermute | solution.py:20
  40.6 1.8 %collective-permute-start.10 = (bf16[64,3072]{1,0:T(8,128)(2,1)S(1)}, bf16[64,3072]{1,0:T(8,128)(2,1)S(1)}, u32[]{:S(2)}, u32[]{:S(2)}) collective-permute-start(bf16[64,3072]{1,0:T(8,128)(2,1)S(1)} %get-tuple-element.34), channel_id=1, source_target_pairs={{0,1},{1,0},{2,3},{3,2},{4,5},{5,4},{6,7},{7,6},{8,9},{9,8},{10,11... | collective-permute-start | bytes 1179656 | tf_op jit(solution)/shard_map/ppermute | solution.py:20
  40.9 5.2 %collective-permute-start.14 = (bf16[64,3072]{1,0:T(8,128)(2,1)S(1)}, bf16[64,3072]{1,0:T(8,128)(2,1)S(1)}, u32[]{:S(2)}, u32[]{:S(2)}) collective-permute-start(bf16[64,3072]{1,0:T(8,128)(2,1)S(1)} %get-tuple-element.36), channel_id=1, source_target_pairs={{0,1},{1,0},{2,3},{3,2},{4,5},{5,4},{6,7},{7,6},{8,9},{9,8},{10,11... | collective-permute-start | bytes 1179656 | tf_op jit(solution)/shard_map/ppermute | solution.py:20
  42.5 6.8 %collective-permute-start.11 = (bf16[16,3072]{1,0:T(8,128)(2,1)S(1)}, bf16[16,3072]{1,0:T(8,128)(2,1)S(1)}, u32[]{:S(2)}, u32[]{:S(2)}) collective-permute-start(bf16[16,3072]{1,0:T(8,128)(2,1)S(1)} %get-tuple-element.44), channel_id=1, source_target_pairs={{0,2},{1,3},{2,0},{3,1},{4,6},{5,7},{6,4},{7,5},{8,10},{9,11},{10,... | collective-permute-start | bytes 294920 | tf_op jit(solution)/shard_map/ppermute | solution.py:20
  43.7 7.1 %collective-permute-start.13 = (bf16[16,3072]{1,0:T(8,128)(2,1)S(1)}, bf16[16,3072]{1,0:T(8,128)(2,1)S(1)}, u32[]{:S(2)}, u32[]{:S(2)}) collective-permute-start(bf16[16,3072]{1,0:T(8,128)(2,1)S(1)} %get-tuple-element.45), channel_id=1, source_target_pairs={{0,18},{1,19},{2,16},{3,17},{4,22},{5,23},{6,20},{7,21},{8,26},{9,... | collective-permute-start | bytes 294920 | tf_op jit(solution)/shard_map/ppermute | solution.py:20
  45.6 6.2 %collective-permute-start.12 = (bf16[16,3072]{1,0:T(8,128)(2,1)S(1)}, bf16[16,3072]{1,0:T(8,128)(2,1)S(1)}, u32[]{:S(2)}, u32[]{:S(2)}) collective-permute-start(bf16[16,3072]{1,0:T(8,128)(2,1)S(1)} %get-tuple-element.46), channel_id=1, source_target_pairs={{0,16},{1,17},{2,18},{3,19},{4,20},{5,21},{6,22},{7,23},{8,24},{9,... | collective-permute-start | bytes 294920 | tf_op jit(solution)/shard_map/ppermute | solution.py:20
  46.2 7.0 %collective-permute-start.15 = (bf16[16,3072]{1,0:T(8,128)(2,1)S(1)}, bf16[16,3072]{1,0:T(8,128)(2,1)S(1)}, u32[]{:S(2)}, u32[]{:S(2)}) collective-permute-start(bf16[16,3072]{1,0:T(8,128)(2,1)S(1)} %get-tuple-element.41), channel_id=1, source_target_pairs={{0,2},{1,3},{2,0},{3,1},{4,6},{5,7},{6,4},{7,5},{8,10},{9,11},{10,... | collective-permute-start | bytes 294920 | tf_op jit(solution)/shard_map/ppermute | solution.py:20
  47.4 7.1 %collective-permute-start.17 = (bf16[16,3072]{1,0:T(8,128)(2,1)S(1)}, bf16[16,3072]{1,0:T(8,128)(2,1)S(1)}, u32[]{:S(2)}, u32[]{:S(2)}) collective-permute-start(bf16[16,3072]{1,0:T(8,128)(2,1)S(1)} %get-tuple-element.42), channel_id=1, source_target_pairs={{0,18},{1,19},{2,16},{3,17},{4,22},{5,23},{6,20},{7,21},{8,26},{9,... | collective-permute-start | bytes 294920 | tf_op jit(solution)/shard_map/ppermute | solution.py:20
  49.4 5.7 %collective-permute-start.16 = (bf16[16,3072]{1,0:T(8,128)(2,1)S(1)}, bf16[16,3072]{1,0:T(8,128)(2,1)S(1)}, u32[]{:S(2)}, u32[]{:S(2)}) collective-permute-start(bf16[16,3072]{1,0:T(8,128)(2,1)S(1)} %get-tuple-element.43), channel_id=1, source_target_pairs={{0,16},{1,17},{2,18},{3,19},{4,20},{5,21},{6,22},{7,23},{8,24},{9,... | collective-permute-start | bytes 294920 | tf_op jit(solution)/shard_map/ppermute | solution.py:20
  55.2 4.2 %collective-permute-start.18 = (bf16[4,6144]{1,0:T(4,128)(2,1)S(1)}, bf16[4,6144]{1,0:T(4,128)(2,1)S(1)}, u32[]{:S(2)}, u32[]{:S(2)}) collective-permute-start(bf16[4,6144]{1,0:T(4,128)(2,1)S(1)} %get-tuple-element.47), channel_id=1, source_target_pairs={{0,4},{1,5},{2,6},{3,7},{4,0},{5,1},{6,2},{7,3},{8,12},{9,13},{10,... | collective-permute-start | bytes 147464 | tf_op jit(solution)/shard_map/ppermute | solution.py:20
  56.7 5.9 %collective-permute-start.20 = (bf16[4,6144]{1,0:T(4,128)(2,1)S(1)}, bf16[4,6144]{1,0:T(4,128)(2,1)S(1)}, u32[]{:S(2)}, u32[]{:S(2)}) collective-permute-start(bf16[4,6144]{1,0:T(4,128)(2,1)S(1)} %get-tuple-element.48), channel_id=1, source_target_pairs={{0,12},{1,13},{2,14},{3,15},{4,8},{5,9},{6,10},{7,11},{8,4},{9,5},... | collective-permute-start | bytes 147464 | tf_op jit(solution)/shard_map/ppermute | solution.py:20
  59.0 5.5 %collective-permute-start.19 = (bf16[4,6144]{1,0:T(4,128)(2,1)S(1)}, bf16[4,6144]{1,0:T(4,128)(2,1)S(1)}, u32[]{:S(2)}, u32[]{:S(2)}) collective-permute-start(bf16[4,6144]{1,0:T(4,128)(2,1)S(1)} %get-tuple-element.49), channel_id=1, source_target_pairs={{0,8},{1,9},{2,10},{3,11},{4,12},{5,13},{6,14},{7,15},{8,0},{9,1},... | collective-permute-start | bytes 147464 | tf_op jit(solution)/shard_map/ppermute | solution.py:20

commit v3 on v2

--- a/solution.py
+++ b/solution.py
@@ -142,13 +142,15 @@
     last = e_count - 1
     resident = [(k, last, 0, half) for k in (0, 1)]
     resident += [(k, e, h, half) for e in range(last) for k in (0, 1) for h in (0, 1)]
-    cut = len(resident) // 2
+    cut = 2
     far = [exchange(packed, *k) for k in far_offsets()]
     units, token = load_only(resident[:cut], packed)
     block = jnp.concatenate([packed] + far, axis=0)
     block, token = lax.optimization_barrier((block, token))
     pieces = [block] + [exchange(block, *k) for k in near_offsets()]
-    more, token = load_only(resident[cut:], block, token)
+    more, token = load_only(resident[cut:5], block, token)
+    units = units + more
+    more, token = load_only(resident[5:], block, token)
     pieces[-1], token = lax.optimization_barrier((pieces[-1], token))
     units = units + more
     pieces = pieces + [exchange(p, 0, 1) for p in pieces]

time: 65.4 us -> 64.9 us (level)
  waiting for transfers between devices: 13.8 us -> 11.1 us
  Pallas kernels: 27.5 us -> 28.6 us
  starting transfers between devices: 22.5 us -> 23.6 us
    ppermute x21, waiting for transfers between devices: 13.8 us -> 11.1 us  [exchange(): return lax.ppermute(x, BOTH, pairs)]
    ppermute x21, starting transfers between devices: 22.5 us -> 23.6 us  [exchange(): return lax.ppermute(x, BOTH, pairs)]
    pallas_call x2 -> x3, Pallas kernels: 12.8 us -> 13.8 us  [stage(): pl.pallas_call(kernel, in_specs=[HBM] * len(used) + [pl.BlockSpec(memory_...]
  transfers between devices with their start and end apart: 21 -> 21, of which waited for: 13 -> 10; matrix products, arithmetic and copies ran while one was open for 0% -> 0% of each run, Pallas kernels for 20% -> 21%
where the time goes in v3:
time: 64.9 us; the launch traced here: 64.7 us
  Pallas kernels  28.6 us (44%)
  starting transfers between devices  23.6 us (36%)
  waiting for transfers between devices  11.1 us (17%)
  other arithmetic  1.09 us (2%)
    ppermute x21, starting transfers between devices, exchange(): return lax.ppermute(x, BOTH, pairs)  23.6 us
    pallas_call x1, Pallas kernels, shards(): pl.pallas_call(kernel, in_specs=[HBM] * 3 + [pl.BlockSpec(memory_space=pl...  13.9 us
    pallas_call x3, Pallas kernels, stage(): pl.pallas_call(kernel, in_specs=[HBM] * len(used) + [pl.BlockSpec(memory_...  13.8 us
    ppermute x21, waiting for transfers between devices, exchange(): return lax.ppermute(x, BOTH, pairs)  11.1 us
  transfers between devices with their start and end apart: 21, of which 10 were waited for; matrix products, arithmetic and copies ran while one was open for 0% of the time, Pallas kernels for 21%

profile of v3, /device:TPU:0, one launch (start us, length us, event | category | flops | bytes accessed | tf_op | source)
XLA Modules:
  0.0 64.7 jit_solution(5935048831228290513)
XLA Ops:
  0.0 0.9 %shard_map.64.refs_2_ = bf16[4,6272]{1,0:T(4,128)(2,1)S(1)} custom-call(bf16[2,4]{1,0:T(2,128)(2,1)} %bitcast.3, s32[2,4]{1,0:T(2,128)} %bitcast.2, bf16[4,6144]{1,0:T(4,128)(2,1)} %tokens_hbm.1), custom_call_target="tpu_custom_call" | custom-call | tf_op jit(solution)/shard_map/pallas_call | solution.py:125
  0.9 5.1 %collective-permute-start.2 = (bf16[4,6272]{1,0:T(4,128)(2,1)S(1)}, bf16[4,6272]{1,0:T(4,128)(2,1)S(1)}, u32[]{:S(2)}, u32[]{:S(2)}) collective-permute-start(bf16[4,6272]{1,0:T(4,128)(2,1)S(1)} %shard_map.64.refs_2_), channel_id=1, source_target_pairs={{0,12},{1,13},{2,14},{3,15},{4,8},{5,9},{6,10},{7,11},{8,4},{9,5},... | collective-permute-start | bytes 150536 | tf_op jit(solution)/shard_map/ppermute | solution.py:20
  6.0 0.0 collective-permute-start.1
  6.0 0.6 collective-permute-start
  6.6 4.6 %shard_map.65 = (bf16[3072,1024]{1,0:T(8,128)(2,1)S(1)}, bf16[3072,1024]{1,0:T(8,128)(2,1)S(1)}, f32[8,128]{1,0:T(8,128)S(1)}) custom-call(bf16[2,6144,1024]{2,1,0:T(8,128)(2,1)} %refs_0_.7, bf16[2,6144,1024]{2,1,0:T(8,128)(2,1)} %refs_1_.5, bf16[4,6272]{1,0:T(4,128)(2,1)S(1)} %shard_map.64.refs_2_), custom_call_target="tpu_custom_call" | custom-call | bytes 12582912 | tf_op jit(solution)/shard_map/pallas_call | solution.py:69
  11.3 0.0 collective-permute-done.2
  11.3 0.0 collective-permute-done.1
  11.3 0.0 collective-permute-done
  11.3 0.1 pad_maximum_fusion.1.refs_2_.refs_1_.refs_4_
  11.4 2.7 %collective-permute-start.3 = (bf16[16,6272]{1,0:T(8,128)(2,1)S(1)}, bf16[16,6272]{1,0:T(8,128)(2,1)S(1)}, u32[]{:S(2)}, u32[]{:S(2)}) collective-permute-start(bf16[16,6272]{1,0:T(8,128)(2,1)S(1)} %pad_maximum_fusion.1.refs_2_.refs_1_.refs_4_), channel_id=1, source_target_pairs={{0,18},{1,19},{2,16},{3,17},{4,22},{5,23},{6,20},{7,21},{8,26},{9,... | collective-permute-start | bytes 602120 | tf_op jit(solution)/shard_map/ppermute | solution.py:20
  14.1 0.5 collective-permute-start.5
  14.6 0.4 collective-permute-start.4
  15.0 0.0 collective-permute-start.6
  15.0 6.4 %shard_map.66 = (bf16[3072,1024]{1,0:T(8,128)(2,1)S(1)}, bf16[3072,1024]{1,0:T(8,128)(2,1)S(1)}, bf16[3072,1024]{1,0:T(8,128)(2,1)S(1)}, f32[8,128]{1,0:T(8,128)S(1)}) custom-call(bf16[2,6144,1024]{2,1,0:T(8,128)(2,1)} %refs_0_.7, bf16[2,6144,1024]{2,1,0:T(8,128)(2,1)} %refs_1_.5, bf16[16,6272]{1,0:T(8,128)(2,1)S(1)} %pad_maximum_fusion.1.refs_2_.refs_1_.refs_4_, ...), custom_call_target="tpu_custom_call" | custom-call | bytes 18874368 | tf_op jit(solution)/shard_map/pallas_call | solution.py:69
  21.4 2.8 %shard_map.67 = (bf16[3072,1024]{1,0:T(8,128)(2,1)S(1)}, f32[8,128]{1,0:T(8,128)S(1)}) custom-call(bf16[2,6144,1024]{2,1,0:T(8,128)(2,1)} %refs_1_.5, bf16[16,6272]{1,0:T(8,128)(2,1)S(1)} %pad_maximum_fusion.1.refs_2_.refs_1_.refs_4_, f32[8,128]{1,0:T(8,128)S(1)} %get-tuple-element.25.refs_2_), custom_call_target="tpu_custom_call" | custom-call | bytes 6291456 | tf_op jit(solution)/shard_map/pallas_call | solution.py:69
  24.2 0.0 copy-start
  24.2 0.0 collective-permute-done.3.refs_7_
  24.2 0.0 collective-permute-done.5.refs_6_
  24.2 0.6 collective-permute-start.8
  24.8 0.0 collective-permute-done.4.refs_5_
  24.8 0.1 collective-permute-start.7
  24.9 0.4 collective-permute-start.9
  25.3 0.0 collective-permute-done.6.refs_8_
  25.3 0.6 collective-permute-done.8.refs_10_
  25.9 0.4 collective-permute-done.7.refs_9_
  26.3 0.3 collective-permute-done.9.refs_11_
  26.6 0.0 copy-done
  26.6 13.9 %shard_map.68 = (bf16[64,3072]{1,0:T(8,128)(2,1)S(1)}, bf16[64,3072]{1,0:T(8,128)(2,1)S(1)}, f32[64,3072]{1,0:T(8,128)S(1)}, f32[64,3072]{1,0:T(8,128)S(1)}, bf1...) custom-call(bf16[2,6144,1024]{2,1,0:T(8,128)(2,1)} %refs_0_.7, ...), custom_call_target="tpu_custom_call", output_to_operand_aliasing={{4}: (14, {}), {5}: (15, {}), {6}: (16, {}), {7}: (17, {})} | custom-call | flops 9663676416 | bytes 50331648 | tf_op jit(solution)/shard_map/pallas_call | solution.py:244
  40.4 0.3 collective-permute-start.10
  40.8 0.2 collective-permute-start.14
  41.0 1.2 %collective-permute-done.10 = bf16[64,3072]{1,0:T(8,128)(2,1)S(1)} collective-permute-done((bf16[64,3072]{1,0:T(8,128)(2,1)S(1)}, bf16[64,3072]{1,0:T(8,128)(2,1)S(1)}, u32[]{:S(2)}, u32[]{:S(2)}) %collective-permute-start.10) | collective-permute-done | bytes 393248 | tf_op jit(solution)/shard_map/ppermute | solution.py:20
  42.2 0.1 fusion.5
  42.4 1.7 %collective-permute-start.11 = (bf16[16,3072]{1,0:T(8,128)(2,1)S(1)}, bf16[16,3072]{1,0:T(8,128)(2,1)S(1)}, u32[]{:S(2)}, u32[]{:S(2)}) collective-permute-start(bf16[16,3072]{1,0:T(8,128)(2,1)S(1)} %get-tuple-element.46), channel_id=1, source_target_pairs={{0,2},{1,3},{2,0},{3,1},{4,6},{5,7},{6,4},{7,5},{8,10},{9,11},{10,... | collective-permute-start | bytes 294920 | tf_op jit(solution)/shard_map/ppermute | solution.py:20
  44.1 1.4 %collective-permute-start.13 = (bf16[16,3072]{1,0:T(8,128)(2,1)S(1)}, bf16[16,3072]{1,0:T(8,128)(2,1)S(1)}, u32[]{:S(2)}, u32[]{:S(2)}) collective-permute-start(bf16[16,3072]{1,0:T(8,128)(2,1)S(1)} %get-tuple-element.47), channel_id=1, source_target_pairs={{0,18},{1,19},{2,16},{3,17},{4,22},{5,23},{6,20},{7,21},{8,26},{9,... | collective-permute-start | bytes 294920 | tf_op jit(solution)/shard_map/ppermute | solution.py:20
  45.5 0.4 collective-permute-start.12
  45.9 0.0 collective-permute-done.14
  45.9 0.1 fusion.4
  46.0 1.7 %collective-permute-start.15 = (bf16[16,3072]{1,0:T(8,128)(2,1)S(1)}, bf16[16,3072]{1,0:T(8,128)(2,1)S(1)}, u32[]{:S(2)}, u32[]{:S(2)}) collective-permute-start(bf16[16,3072]{1,0:T(8,128)(2,1)S(1)} %get-tuple-element.43), channel_id=1, source_target_pairs={{0,2},{1,3},{2,0},{3,1},{4,6},{5,7},{6,4},{7,5},{8,10},{9,11},{10,... | collective-permute-start | bytes 294920 | tf_op jit(solution)/shard_map/ppermute | solution.py:20
  47.7 1.4 %collective-permute-start.17 = (bf16[16,3072]{1,0:T(8,128)(2,1)S(1)}, bf16[16,3072]{1,0:T(8,128)(2,1)S(1)}, u32[]{:S(2)}, u32[]{:S(2)}) collective-permute-start(bf16[16,3072]{1,0:T(8,128)(2,1)S(1)} %get-tuple-element.44), channel_id=1, source_target_pairs={{0,18},{1,19},{2,16},{3,17},{4,22},{5,23},{6,20},{7,21},{8,26},{9,... | collective-permute-start | bytes 294920 | tf_op jit(solution)/shard_map/ppermute | solution.py:20
  49.2 0.0 collective-permute-done.11
  49.2 1.6 %collective-permute-start.16 = (bf16[16,3072]{1,0:T(8,128)(2,1)S(1)}, bf16[16,3072]{1,0:T(8,128)(2,1)S(1)}, u32[]{:S(2)}, u32[]{:S(2)}) collective-permute-start(bf16[16,3072]{1,0:T(8,128)(2,1)S(1)} %get-tuple-element.45), channel_id=1, source_target_pairs={{0,16},{1,17},{2,18},{3,19},{4,20},{5,21},{6,22},{7,23},{8,24},{9,... | collective-permute-start | bytes 294920 | tf_op jit(solution)/shard_map/ppermute | solution.py:20
  50.8 0.0 collective-permute-done.13
  50.8 0.7 %collective-permute-done.12 = bf16[16,3072]{1,0:T(8,128)(2,1)S(1)} collective-permute-done((bf16[16,3072]{1,0:T(8,128)(2,1)S(1)}, bf16[16,3072]{1,0:T(8,128)(2,1)S(1)}, u32[]{:S(2)}, u32[]{:S(2)}) %collective-permute-start.12) | collective-permute-done | bytes 98336 | tf_op jit(solution)/shard_map/ppermute | solution.py:20
  51.6 1.4 %collective-permute-done.15 = bf16[16,3072]{1,0:T(8,128)(2,1)S(1)} collective-permute-done((bf16[16,3072]{1,0:T(8,128)(2,1)S(1)}, bf16[16,3072]{1,0:T(8,128)(2,1)S(1)}, u32[]{:S(2)}, u32[]{:S(2)}) %collective-permute-start.15) | collective-permute-done | bytes 98336 | tf_op jit(solution)/shard_map/ppermute | solution.py:20
  52.9 1.8 %collective-permute-done.17 = bf16[16,3072]{1,0:T(8,128)(2,1)S(1)} collective-permute-done((bf16[16,3072]{1,0:T(8,128)(2,1)S(1)}, bf16[16,3072]{1,0:T(8,128)(2,1)S(1)}, u32[]{:S(2)}, u32[]{:S(2)}) %collective-permute-start.17) | collective-permute-done | bytes 98336 | tf_op jit(solution)/shard_map/ppermute | solution.py:20
  54.8 0.2 collective-permute-done.16
  55.0 0.1 fusion.8
  55.1 1.5 %collective-permute-start.18 = (bf16[4,6144]{1,0:T(4,128)(2,1)S(1)}, bf16[4,6144]{1,0:T(4,128)(2,1)S(1)}, u32[]{:S(2)}, u32[]{:S(2)}) collective-permute-start(bf16[4,6144]{1,0:T(4,128)(2,1)S(1)} %get-tuple-element.49), channel_id=1, source_target_pairs={{0,4},{1,5},{2,6},{3,7},{4,0},{5,1},{6,2},{7,3},{8,12},{9,13},{10,... | collective-permute-start | bytes 147464 | tf_op jit(solution)/shard_map/ppermute | solution.py:20
  56.6 2.4 %collective-permute-start.20 = (bf16[4,6144]{1,0:T(4,128)(2,1)S(1)}, bf16[4,6144]{1,0:T(4,128)(2,1)S(1)}, u32[]{:S(2)}, u32[]{:S(2)}) collective-permute-start(bf16[4,6144]{1,0:T(4,128)(2,1)S(1)} %get-tuple-element.50), channel_id=1, source_target_pairs={{0,12},{1,13},{2,14},{3,15},{4,8},{5,9},{6,10},{7,11},{8,4},{9,5},... | collective-permute-start | bytes 147464 | tf_op jit(solution)/shard_map/ppermute | solution.py:20
  59.0 0.5 collective-permute-start.19
  59.5 0.0 collective-permute-done.18
  59.5 3.2 %collective-permute-done.20 = bf16[4,6144]{1,0:T(4,128)(2,1)S(1)} collective-permute-done((bf16[4,6144]{1,0:T(4,128)(2,1)S(1)}, bf16[4,6144]{1,0:T(4,128)(2,1)S(1)}, u32[]{:S(2)}, u32[]{:S(2)}) %collective-permute-start.20) | collective-permute-done | bytes 49184 | tf_op jit(solution)/shard_map/ppermute | solution.py:20
  62.7 1.3 %collective-permute-done.19 = bf16[4,6144]{1,0:T(4,128)(2,1)S(1)} collective-permute-done((bf16[4,6144]{1,0:T(4,128)(2,1)S(1)}, bf16[4,6144]{1,0:T(4,128)(2,1)S(1)}, u32[]{:S(2)}, u32[]{:S(2)}) %collective-permute-start.19) | collective-permute-done | bytes 49184 | tf_op jit(solution)/shard_map/ppermute | solution.py:20
  64.0 0.7 %fusion.3 = bf16[4,6144]{1,0:T(4,128)(2,1)} fusion(f32[16,3072]{1,0:T(8,128)S(1)} %slice_add_fusion.1, f32[16,3072]{1,0:T(8,128)S(1)} %slice_add_fusion, bf16[4,6144]{1,0:T(4,128)(2,1)S(1)} %collective-permute-done.20, bf16[4,6144]{1,0:T(4,128)(2,1)S(1)} %collective-permute-done.19, bf16[4,6144]{1,0:T(4,128)(2,1)S(1)} %collective-permute-done.18), kind=kLoop, calls=%fused_computation.11 | loop fusion | flops 196608 | bytes 589824 | tf_op jit(solution)/shard_map/convert_element_type | solution.py:280
  (5 shorter events, 0.2 us)
Async XLA Ops:
  0.9 10.4 %collective-permute-start.2 = (bf16[4,6272]{1,0:T(4,128)(2,1)S(1)}, bf16[4,6272]{1,0:T(4,128)(2,1)S(1)}, u32[]{:S(2)}, u32[]{:S(2)}) collective-permute-start(bf16[4,6272]{1,0:T(4,128)(2,1)S(1)} %shard_map.64.refs_2_), channel_id=1, source_target_pairs={{0,12},{1,13},{2,14},{3,15},{4,8},{5,9},{6,10},{7,11},{8,4},{9,5},... | collective-permute-start | bytes 150536 | tf_op jit(solution)/shard_map/ppermute | solution.py:20
  6.0 5.3 %collective-permute-start.1 = (bf16[4,6272]{1,0:T(4,128)(2,1)S(1)}, bf16[4,6272]{1,0:T(4,128)(2,1)S(1)}, u32[]{:S(2)}, u32[]{:S(2)}) collective-permute-start(bf16[4,6272]{1,0:T(4,128)(2,1)S(1)} %shard_map.64.refs_2_), channel_id=1, source_target_pairs={{0,8},{1,9},{2,10},{3,11},{4,12},{5,13},{6,14},{7,15},{8,0},{9,1},... | collective-permute-start | bytes 150536 | tf_op jit(solution)/shard_map/ppermute | solution.py:20
  6.0 5.3 %collective-permute-start = (bf16[4,6272]{1,0:T(4,128)(2,1)S(1)}, bf16[4,6272]{1,0:T(4,128)(2,1)S(1)}, u32[]{:S(2)}, u32[]{:S(2)}) collective-permute-start(bf16[4,6272]{1,0:T(4,128)(2,1)S(1)} %shard_map.64.refs_2_), channel_id=1, source_target_pairs={{0,4},{1,5},{2,6},{3,7},{4,0},{5,1},{6,2},{7,3},{8,12},{9,13},{10,... | collective-permute-start | bytes 150536 | tf_op jit(solution)/shard_map/ppermute | solution.py:20
  11.4 12.8 %collective-permute-start.3 = (bf16[16,6272]{1,0:T(8,128)(2,1)S(1)}, bf16[16,6272]{1,0:T(8,128)(2,1)S(1)}, u32[]{:S(2)}, u32[]{:S(2)}) collective-permute-start(bf16[16,6272]{1,0:T(8,128)(2,1)S(1)} %pad_maximum_fusion.1.refs_2_.refs_1_.refs_4_), channel_id=1, source_target_pairs={{0,18},{1,19},{2,16},{3,17},{4,22},{5,23},{6,20},{7,21},{8,26},{9,... | collective-permute-start | bytes 602120 | tf_op jit(solution)/shard_map/ppermute | solution.py:20
  14.1 10.2 %collective-permute-start.5 = (bf16[16,6272]{1,0:T(8,128)(2,1)S(1)}, bf16[16,6272]{1,0:T(8,128)(2,1)S(1)}, u32[]{:S(2)}, u32[]{:S(2)}) collective-permute-start(bf16[16,6272]{1,0:T(8,128)(2,1)S(1)} %pad_maximum_fusion.1.refs_2_.refs_1_.refs_4_), channel_id=1, source_target_pairs={{0,16},{1,17},{2,18},{3,19},{4,20},{5,21},{6,22},{7,23},{8,24},{9,... | collective-permute-start | bytes 602120 | tf_op jit(solution)/shard_map/ppermute | solution.py:20
  14.6 10.2 %collective-permute-start.4 = (bf16[16,6272]{1,0:T(8,128)(2,1)S(1)}, bf16[16,6272]{1,0:T(8,128)(2,1)S(1)}, u32[]{:S(2)}, u32[]{:S(2)}) collective-permute-start(bf16[16,6272]{1,0:T(8,128)(2,1)S(1)} %pad_maximum_fusion.1.refs_2_.refs_1_.refs_4_), channel_id=1, source_target_pairs={{0,2},{1,3},{2,0},{3,1},{4,6},{5,7},{6,4},{7,5},{8,10},{9,11},{10,... | collective-permute-start | bytes 602120 | tf_op jit(solution)/shard_map/ppermute | solution.py:20
  15.0 10.4 %collective-permute-start.6 = (bf16[16,6272]{1,0:T(8,128)(2,1)S(1)}, bf16[16,6272]{1,0:T(8,128)(2,1)S(1)}, u32[]{:S(2)}, u32[]{:S(2)}) collective-permute-start(bf16[16,6272]{1,0:T(8,128)(2,1)S(1)} %pad_maximum_fusion.1.refs_2_.refs_1_.refs_4_), channel_id=1, source_target_pairs={{0,1},{1,0},{2,3},{3,2},{4,5},{5,4},{6,7},{7,6},{8,9},{9,8},{10,11... | collective-permute-start | bytes 602120 | tf_op jit(solution)/shard_map/ppermute | solution.py:20
  24.2 2.3 %copy-start = (f32[8,128]{1,0:T(8,128)}, f32[8,128]{1,0:T(8,128)S(1)}, u32[]{:S(2)}) copy-start(f32[8,128]{1,0:T(8,128)S(1)} %get-tuple-element.27.refs_3_) | copy-start | bytes 12292
  24.2 1.6 %collective-permute-start.8 = (bf16[16,6272]{1,0:T(8,128)(2,1)S(1)}, bf16[16,6272]{1,0:T(8,128)(2,1)S(1)}, u32[]{:S(2)}, u32[]{:S(2)}) collective-permute-start(bf16[16,6272]{1,0:T(8,128)(2,1)S(1)} %collective-permute-done.5.refs_6_), channel_id=1, source_target_pairs={{0,1},{1,0},{2,3},{3,2},{4,5},{5,4},{6,7},{7,6},{8,9},{9,8},{10,11... | collective-permute-start | bytes 602120 | tf_op jit(solution)/shard_map/ppermute | solution.py:20
  24.8 1.4 %collective-permute-start.7 = (bf16[16,6272]{1,0:T(8,128)(2,1)S(1)}, bf16[16,6272]{1,0:T(8,128)(2,1)S(1)}, u32[]{:S(2)}, u32[]{:S(2)}) collective-permute-start(bf16[16,6272]{1,0:T(8,128)(2,1)S(1)} %collective-permute-done.4.refs_5_), channel_id=1, source_target_pairs={{0,1},{1,0},{2,3},{3,2},{4,5},{5,4},{6,7},{7,6},{8,9},{9,8},{10,11... | collective-permute-start | bytes 602120 | tf_op jit(solution)/shard_map/ppermute | solution.py:20
  24.9 1.6 %collective-permute-start.9 = (bf16[16,6272]{1,0:T(8,128)(2,1)S(1)}, bf16[16,6272]{1,0:T(8,128)(2,1)S(1)}, u32[]{:S(2)}, u32[]{:S(2)}) collective-permute-start(bf16[16,6272]{1,0:T(8,128)(2,1)S(1)} %collective-permute-done.3.refs_7_), channel_id=1, source_target_pairs={{0,1},{1,0},{2,3},{3,2},{4,5},{5,4},{6,7},{7,6},{8,9},{9,8},{10,11... | collective-permute-start | bytes 602120 | tf_op jit(solution)/shard_map/ppermute | solution.py:20
  40.4 1.8 %collective-permute-start.10 = (bf16[64,3072]{1,0:T(8,128)(2,1)S(1)}, bf16[64,3072]{1,0:T(8,128)(2,1)S(1)}, u32[]{:S(2)}, u32[]{:S(2)}) collective-permute-start(bf16[64,3072]{1,0:T(8,128)(2,1)S(1)} %get-tuple-element.36), channel_id=1, source_target_pairs={{0,1},{1,0},{2,3},{3,2},{4,5},{5,4},{6,7},{7,6},{8,9},{9,8},{10,11... | collective-permute-start | bytes 1179656 | tf_op jit(solution)/shard_map/ppermute | solution.py:20
  40.8 5.1 %collective-permute-start.14 = (bf16[64,3072]{1,0:T(8,128)(2,1)S(1)}, bf16[64,3072]{1,0:T(8,128)(2,1)S(1)}, u32[]{:S(2)}, u32[]{:S(2)}) collective-permute-start(bf16[64,3072]{1,0:T(8,128)(2,1)S(1)} %get-tuple-element.38), channel_id=1, source_target_pairs={{0,1},{1,0},{2,3},{3,2},{4,5},{5,4},{6,7},{7,6},{8,9},{9,8},{10,11... | collective-permute-start | bytes 1179656 | tf_op jit(solution)/shard_map/ppermute | solution.py:20
  42.4 6.8 %collective-permute-start.11 = (bf16[16,3072]{1,0:T(8,128)(2,1)S(1)}, bf16[16,3072]{1,0:T(8,128)(2,1)S(1)}, u32[]{:S(2)}, u32[]{:S(2)}) collective-permute-start(bf16[16,3072]{1,0:T(8,128)(2,1)S(1)} %get-tuple-element.46), channel_id=1, source_target_pairs={{0,2},{1,3},{2,0},{3,1},{4,6},{5,7},{6,4},{7,5},{8,10},{9,11},{10,... | collective-permute-start | bytes 294920 | tf_op jit(solution)/shard_map/ppermute | solution.py:20
  44.1 6.7 %collective-permute-start.13 = (bf16[16,3072]{1,0:T(8,128)(2,1)S(1)}, bf16[16,3072]{1,0:T(8,128)(2,1)S(1)}, u32[]{:S(2)}, u32[]{:S(2)}) collective-permute-start(bf16[16,3072]{1,0:T(8,128)(2,1)S(1)} %get-tuple-element.47), channel_id=1, source_target_pairs={{0,18},{1,19},{2,16},{3,17},{4,22},{5,23},{6,20},{7,21},{8,26},{9,... | collective-permute-start | bytes 294920 | tf_op jit(solution)/shard_map/ppermute | solution.py:20
  45.5 6.0 %collective-permute-start.12 = (bf16[16,3072]{1,0:T(8,128)(2,1)S(1)}, bf16[16,3072]{1,0:T(8,128)(2,1)S(1)}, u32[]{:S(2)}, u32[]{:S(2)}) collective-permute-start(bf16[16,3072]{1,0:T(8,128)(2,1)S(1)} %get-tuple-element.48), channel_id=1, source_target_pairs={{0,16},{1,17},{2,18},{3,19},{4,20},{5,21},{6,22},{7,23},{8,24},{9,... | collective-permute-start | bytes 294920 | tf_op jit(solution)/shard_map/ppermute | solution.py:20
  46.0 6.9 %collective-permute-start.15 = (bf16[16,3072]{1,0:T(8,128)(2,1)S(1)}, bf16[16,3072]{1,0:T(8,128)(2,1)S(1)}, u32[]{:S(2)}, u32[]{:S(2)}) collective-permute-start(bf16[16,3072]{1,0:T(8,128)(2,1)S(1)} %get-tuple-element.43), channel_id=1, source_target_pairs={{0,2},{1,3},{2,0},{3,1},{4,6},{5,7},{6,4},{7,5},{8,10},{9,11},{10,... | collective-permute-start | bytes 294920 | tf_op jit(solution)/shard_map/ppermute | solution.py:20
  47.7 7.0 %collective-permute-start.17 = (bf16[16,3072]{1,0:T(8,128)(2,1)S(1)}, bf16[16,3072]{1,0:T(8,128)(2,1)S(1)}, u32[]{:S(2)}, u32[]{:S(2)}) collective-permute-start(bf16[16,3072]{1,0:T(8,128)(2,1)S(1)} %get-tuple-element.44), channel_id=1, source_target_pairs={{0,18},{1,19},{2,16},{3,17},{4,22},{5,23},{6,20},{7,21},{8,26},{9,... | collective-permute-start | bytes 294920 | tf_op jit(solution)/shard_map/ppermute | solution.py:20
  49.2 5.7 %collective-permute-start.16 = (bf16[16,3072]{1,0:T(8,128)(2,1)S(1)}, bf16[16,3072]{1,0:T(8,128)(2,1)S(1)}, u32[]{:S(2)}, u32[]{:S(2)}) collective-permute-start(bf16[16,3072]{1,0:T(8,128)(2,1)S(1)} %get-tuple-element.45), channel_id=1, source_target_pairs={{0,16},{1,17},{2,18},{3,19},{4,20},{5,21},{6,22},{7,23},{8,24},{9,... | collective-permute-start | bytes 294920 | tf_op jit(solution)/shard_map/ppermute | solution.py:20
  55.1 4.4 %collective-permute-start.18 = (bf16[4,6144]{1,0:T(4,128)(2,1)S(1)}, bf16[4,6144]{1,0:T(4,128)(2,1)S(1)}, u32[]{:S(2)}, u32[]{:S(2)}) collective-permute-start(bf16[4,6144]{1,0:T(4,128)(2,1)S(1)} %get-tuple-element.49), channel_id=1, source_target_pairs={{0,4},{1,5},{2,6},{3,7},{4,0},{5,1},{6,2},{7,3},{8,12},{9,13},{10,... | collective-permute-start | bytes 147464 | tf_op jit(solution)/shard_map/ppermute | solution.py:20
  56.6 6.2 %collective-permute-start.20 = (bf16[4,6144]{1,0:T(4,128)(2,1)S(1)}, bf16[4,6144]{1,0:T(4,128)(2,1)S(1)}, u32[]{:S(2)}, u32[]{:S(2)}) collective-permute-start(bf16[4,6144]{1,0:T(4,128)(2,1)S(1)} %get-tuple-element.50), channel_id=1, source_target_pairs={{0,12},{1,13},{2,14},{3,15},{4,8},{5,9},{6,10},{7,11},{8,4},{9,5},... | collective-permute-start | bytes 147464 | tf_op jit(solution)/shard_map/ppermute | solution.py:20
  59.0 5.0 %collective-permute-start.19 = (bf16[4,6144]{1,0:T(4,128)(2,1)S(1)}, bf16[4,6144]{1,0:T(4,128)(2,1)S(1)}, u32[]{:S(2)}, u32[]{:S(2)}) collective-permute-start(bf16[4,6144]{1,0:T(4,128)(2,1)S(1)} %get-tuple-element.51), channel_id=1, source_target_pairs={{0,8},{1,9},{2,10},{3,11},{4,12},{5,13},{6,14},{7,15},{8,0},{9,1},... | collective-permute-start | bytes 147464 | tf_op jit(solution)/shard_map/ppermute | solution.py:20

commit v4 on v3

--- a/solution.py
+++ b/solution.py
@@ -21,11 +21,11 @@
 
 
 def near_offsets():
-    return [(e, y) for e in range(lax.axis_size("expert")) for y in (0, 2)][1:]
+    return [(e, y) for e in range(lax.axis_size("expert")) for y in (0, 2)][:0:-1]
 
 
 def far_offsets():
-    return [(0, 4 * k) for k in range(1, lax.axis_size("tensor") // 4)]
+    return [(0, 4 * k) for k in range(lax.axis_size("tensor") // 4 - 1, 0, -1)]
 
 
 def in_vmem(x):
@@ -186,17 +186,22 @@
         for copy in tails:
             copy.start()
         me = lax.axis_index("expert")
-        for i, ref in enumerate(xrefs):
-            r = slice(i * rows, (i + 1) * rows)
-            xs[r, :] = ref[:, LANES:]
-            meta = ref[:, :LANES].astype(jnp.float32)
-            for e in range(e_count):
-                expert = (me * e_count + e).astype(jnp.float32)
-                col = sum(
-                    jnp.where(meta[:, top + i : top + i + 1] == expert, meta[:, i : i + 1], 0.0)
-                    for i in range(top)
-                )
-                gate_ref[e, r, :] = jnp.broadcast_to(col, meta.shape)
+
+        def fill():
+            for i, ref in enumerate(xrefs):
+                xs[i * rows : (i + 1) * rows, :] = ref[:, LANES:]
+
+        def weigh():
+            for i, ref in enumerate(xrefs):
+                r = slice(i * rows, (i + 1) * rows)
+                meta = ref[:, :LANES].astype(jnp.float32)
+                for e in range(e_count):
+                    expert = (me * e_count + e).astype(jnp.float32)
+                    col = sum(
+                        jnp.where(meta[:, top + i : top + i + 1] == expert, meta[:, i : i + 1], 0.0)
+                        for i in range(top)
+                    )
+                    gate_ref[e, r, :] = jnp.broadcast_to(col, meta.shape)
 
         for e in range(e_count):
             def part(k, h):
@@ -211,14 +216,16 @@
                 u = dot(xs[:, :half], part(1, 0)[:, c]) + dot(xs[:, half:], part(1, 1)[:, c])
                 h_ref[e, :, c] = (g / (1.0 + jnp.exp(-g)) * u).astype(jnp.bfloat16)
 
-            if e < last:
+            if e == 0:
 
                 @pl.when(me >= 0)
                 def _():
+                    fill()
                     columns(f, fb, hide)
             else:
+                if e == last:
+                    weigh()
                 columns(f, fb, hide)
-
             if e == 0:
                 for copy in downs:
                     copy.start()
@@ -230,7 +237,7 @@
             side, start = divmod(j * chunk, d // SIDES)
 
             def out(c):
-                s = sum(dot(h_ref[e], views[e][:, c]) * gate_ref[e, :, 0:1] for e in range(e_count))
+                s = sum(dot(h_ref[e], views[e][:, c]) * jnp.concatenate([gate_ref[e]] * (256 // LANES), axis=1) for e in range(e_count))
                 to = slice(c.start + start, c.stop + start)
                 keeps[side][:, to] = s[: total // 2]
                 sends[side][:, to] = s[total // 2 :].astype(jnp.bfloat16)

time: 64.9 us -> 64.3 us (level)
  transfers between devices with their start and end apart: 21 -> 21, of which waited for: 10 -> 12; matrix products, arithmetic and copies ran while one was open for 0% -> 0% of each run, Pallas kernels for 21% -> 22%
where the time goes in v4:
time: 64.3 us; the launch traced here: 64.1 us
  Pallas kernels  28.3 us (44%)
  starting transfers between devices  23.3 us (36%)
  waiting for transfers between devices  11.1 us (17%)
  other arithmetic  1.09 us (2%)
    ppermute x21, starting transfers between devices, exchange(): return lax.ppermute(x, BOTH, pairs)  23.3 us
    pallas_call x3, Pallas kernels, stage(): pl.pallas_call(kernel, in_specs=[HBM] * len(used) + [pl.BlockSpec(memory_...  13.8 us
    pallas_call x1, Pallas kernels, shards(): pl.pallas_call(kernel, in_specs=[HBM] * 3 + [pl.BlockSpec(memory_space=pl...  13.6 us
    ppermute x21, waiting for transfers between devices, exchange(): return lax.ppermute(x, BOTH, pairs)  11.1 us
  transfers between devices with their start and end apart: 21, of which 12 were waited for; matrix products, arithmetic and copies ran while one was open for 0% of the time, Pallas kernels for 22%

profile of v4, /device:TPU:0, one launch (start us, length us, event | category | flops | bytes accessed | tf_op | source)
XLA Modules:
  0.0 64.1 jit_solution(1414519021170543103)
XLA Ops:
  0.0 0.9 %shard_map.64.refs_2_ = bf16[4,6272]{1,0:T(4,128)(2,1)S(1)} custom-call(bf16[2,4]{1,0:T(2,128)(2,1)} %bitcast.3, s32[2,4]{1,0:T(2,128)} %bitcast.2, bf16[4,6144]{1,0:T(4,128)(2,1)} %tokens_hbm.1), custom_call_target="tpu_custom_call" | custom-call | tf_op jit(solution)/shard_map/pallas_call | solution.py:125
  0.9 3.1 %collective-permute-start.2 = (bf16[4,6272]{1,0:T(4,128)(2,1)S(1)}, bf16[4,6272]{1,0:T(4,128)(2,1)S(1)}, u32[]{:S(2)}, u32[]{:S(2)}) collective-permute-start(bf16[4,6272]{1,0:T(4,128)(2,1)S(1)} %shard_map.64.refs_2_), channel_id=1, source_target_pairs={{0,4},{1,5},{2,6},{3,7},{4,0},{5,1},{6,2},{7,3},{8,12},{9,13},{10,... | collective-permute-start | bytes 150536 | tf_op jit(solution)/shard_map/ppermute | solution.py:20
  4.0 2.6 %collective-permute-start.1 = (bf16[4,6272]{1,0:T(4,128)(2,1)S(1)}, bf16[4,6272]{1,0:T(4,128)(2,1)S(1)}, u32[]{:S(2)}, u32[]{:S(2)}) collective-permute-start(bf16[4,6272]{1,0:T(4,128)(2,1)S(1)} %shard_map.64.refs_2_), channel_id=1, source_target_pairs={{0,8},{1,9},{2,10},{3,11},{4,12},{5,13},{6,14},{7,15},{8,0},{9,1},... | collective-permute-start | bytes 150536 | tf_op jit(solution)/shard_map/ppermute | solution.py:20
  6.5 0.0 collective-permute-start
  6.5 4.6 %shard_map.65 = (bf16[3072,1024]{1,0:T(8,128)(2,1)S(1)}, bf16[3072,1024]{1,0:T(8,128)(2,1)S(1)}, f32[8,128]{1,0:T(8,128)S(1)}) custom-call(bf16[2,6144,1024]{2,1,0:T(8,128)(2,1)} %refs_0_.7, bf16[2,6144,1024]{2,1,0:T(8,128)(2,1)} %refs_1_.5, bf16[4,6272]{1,0:T(4,128)(2,1)S(1)} %shard_map.64.refs_2_), custom_call_target="tpu_custom_call" | custom-call | bytes 12582912 | tf_op jit(solution)/shard_map/pallas_call | solution.py:69
  11.2 0.0 collective-permute-done.2
  11.2 0.0 collective-permute-done.1
  11.2 1.2 %collective-permute-done = bf16[4,6272]{1,0:T(4,128)(2,1)S(1)} collective-permute-done((bf16[4,6272]{1,0:T(4,128)(2,1)S(1)}, bf16[4,6272]{1,0:T(4,128)(2,1)S(1)}, u32[]{:S(2)}, u32[]{:S(2)}) %collective-permute-start) | collective-permute-done | bytes 50208 | tf_op jit(solution)/shard_map/ppermute | solution.py:20
  12.4 0.1 pad_maximum_fusion.1.refs_2_.refs_1_.refs_4_
  12.6 1.6 %collective-permute-start.3 = (bf16[16,6272]{1,0:T(8,128)(2,1)S(1)}, bf16[16,6272]{1,0:T(8,128)(2,1)S(1)}, u32[]{:S(2)}, u32[]{:S(2)}) collective-permute-start(bf16[16,6272]{1,0:T(8,128)(2,1)S(1)} %pad_maximum_fusion.1.refs_2_.refs_1_.refs_4_), channel_id=1, source_target_pairs={{0,2},{1,3},{2,0},{3,1},{4,6},{5,7},{6,4},{7,5},{8,10},{9,11},{10,... | collective-permute-start | bytes 602120 | tf_op jit(solution)/shard_map/ppermute | solution.py:20
  14.2 1.5 %collective-permute-start.5 = (bf16[16,6272]{1,0:T(8,128)(2,1)S(1)}, bf16[16,6272]{1,0:T(8,128)(2,1)S(1)}, u32[]{:S(2)}, u32[]{:S(2)}) collective-permute-start(bf16[16,6272]{1,0:T(8,128)(2,1)S(1)} %pad_maximum_fusion.1.refs_2_.refs_1_.refs_4_), channel_id=1, source_target_pairs={{0,16},{1,17},{2,18},{3,19},{4,20},{5,21},{6,22},{7,23},{8,24},{9,... | collective-permute-start | bytes 602120 | tf_op jit(solution)/shard_map/ppermute | solution.py:20
  15.6 0.5 collective-permute-start.4
  16.1 0.0 collective-permute-start.6
  16.1 6.4 %shard_map.66 = (bf16[3072,1024]{1,0:T(8,128)(2,1)S(1)}, bf16[3072,1024]{1,0:T(8,128)(2,1)S(1)}, bf16[3072,1024]{1,0:T(8,128)(2,1)S(1)}, f32[8,128]{1,0:T(8,128)S(1)}) custom-call(bf16[2,6144,1024]{2,1,0:T(8,128)(2,1)} %refs_0_.7, bf16[2,6144,1024]{2,1,0:T(8,128)(2,1)} %refs_1_.5, bf16[16,6272]{1,0:T(8,128)(2,1)S(1)} %pad_maximum_fusion.1.refs_2_.refs_1_.refs_4_, ...), custom_call_target="tpu_custom_call" | custom-call | bytes 18874368 | tf_op jit(solution)/shard_map/pallas_call | solution.py:69
  22.6 2.8 %shard_map.67 = (bf16[3072,1024]{1,0:T(8,128)(2,1)S(1)}, f32[8,128]{1,0:T(8,128)S(1)}) custom-call(bf16[2,6144,1024]{2,1,0:T(8,128)(2,1)} %refs_1_.5, bf16[16,6272]{1,0:T(8,128)(2,1)S(1)} %pad_maximum_fusion.1.refs_2_.refs_1_.refs_4_, f32[8,128]{1,0:T(8,128)S(1)} %get-tuple-element.25.refs_2_), custom_call_target="tpu_custom_call" | custom-call | bytes 6291456 | tf_op jit(solution)/shard_map/pallas_call | solution.py:69
  25.4 0.0 copy-start
  25.4 0.0 collective-permute-done.3.refs_7_
  25.4 0.0 collective-permute-done.5.refs_6_
  25.4 0.6 collective-permute-start.8
  26.0 0.0 collective-permute-done.4.refs_5_
  26.0 0.1 collective-permute-start.7
  26.1 0.4 collective-permute-start.9
  26.5 0.0 collective-permute-done.6.refs_8_
  26.5 0.6 collective-permute-done.8.refs_10_
  27.0 0.4 collective-permute-done.7.refs_9_
  27.4 0.3 collective-permute-done.9.refs_11_
  27.7 0.0 copy-done
  27.7 13.6 %shard_map.68 = (bf16[64,3072]{1,0:T(8,128)(2,1)S(1)}, bf16[64,3072]{1,0:T(8,128)(2,1)S(1)}, f32[64,3072]{1,0:T(8,128)S(1)}, f32[64,3072]{1,0:T(8,128)S(1)}, bf1...) custom-call(bf16[2,6144,1024]{2,1,0:T(8,128)(2,1)} %refs_0_.7, ...), custom_call_target="tpu_custom_call", output_to_operand_aliasing={{4}: (14, {}), {5}: (15, {}), {6}: (16, {}), {7}: (17, {})} | custom-call | flops 9663676416 | bytes 50331648 | tf_op jit(solution)/shard_map/pallas_call | solution.py:251
  41.4 0.3 collective-permute-start.10
  41.7 0.2 collective-permute-start.14
  41.9 1.2 %collective-permute-done.10 = bf16[64,3072]{1,0:T(8,128)(2,1)S(1)} collective-permute-done((bf16[64,3072]{1,0:T(8,128)(2,1)S(1)}, bf16[64,3072]{1,0:T(8,128)(2,1)S(1)}, u32[]{:S(2)}, u32[]{:S(2)}) %collective-permute-start.10) | collective-permute-done | bytes 393248 | tf_op jit(solution)/shard_map/ppermute | solution.py:20
  43.1 0.1 fusion.5
  43.3 2.5 %collective-permute-start.11 = (bf16[16,3072]{1,0:T(8,128)(2,1)S(1)}, bf16[16,3072]{1,0:T(8,128)(2,1)S(1)}, u32[]{:S(2)}, u32[]{:S(2)}) collective-permute-start(bf16[16,3072]{1,0:T(8,128)(2,1)S(1)} %get-tuple-element.46), channel_id=1, source_target_pairs={{0,18},{1,19},{2,16},{3,17},{4,22},{5,23},{6,20},{7,21},{8,26},{9,... | collective-permute-start | bytes 294920 | tf_op jit(solution)/shard_map/ppermute | solution.py:20
  45.8 0.5 collective-permute-start.13
  46.3 0.5 collective-permute-start.12
  46.8 0.0 collective-permute-done.14
  46.8 0.1 fusion.4
  47.0 2.5 %collective-permute-start.15 = (bf16[16,3072]{1,0:T(8,128)(2,1)S(1)}, bf16[16,3072]{1,0:T(8,128)(2,1)S(1)}, u32[]{:S(2)}, u32[]{:S(2)}) collective-permute-start(bf16[16,3072]{1,0:T(8,128)(2,1)S(1)} %get-tuple-element.43), channel_id=1, source_target_pairs={{0,18},{1,19},{2,16},{3,17},{4,22},{5,23},{6,20},{7,21},{8,26},{9,... | collective-permute-start | bytes 294920 | tf_op jit(solution)/shard_map/ppermute | solution.py:20
  49.5 0.5 collective-permute-start.17
  50.0 0.0 collective-permute-done.11
  50.0 1.3 %collective-permute-start.16 = (bf16[16,3072]{1,0:T(8,128)(2,1)S(1)}, bf16[16,3072]{1,0:T(8,128)(2,1)S(1)}, u32[]{:S(2)}, u32[]{:S(2)}) collective-permute-start(bf16[16,3072]{1,0:T(8,128)(2,1)S(1)} %get-tuple-element.45), channel_id=1, source_target_pairs={{0,16},{1,17},{2,18},{3,19},{4,20},{5,21},{6,22},{7,23},{8,24},{9,... | collective-permute-start | bytes 294920 | tf_op jit(solution)/shard_map/ppermute | solution.py:20
  51.3 1.2 %collective-permute-done.13 = bf16[16,3072]{1,0:T(8,128)(2,1)S(1)} collective-permute-done((bf16[16,3072]{1,0:T(8,128)(2,1)S(1)}, bf16[16,3072]{1,0:T(8,128)(2,1)S(1)}, u32[]{:S(2)}, u32[]{:S(2)}) %collective-permute-start.13) | collective-permute-done | bytes 98336 | tf_op jit(solution)/shard_map/ppermute | solution.py:20
  52.5 0.0 collective-permute-done.12
  52.6 2.4 %collective-permute-done.15 = bf16[16,3072]{1,0:T(8,128)(2,1)S(1)} collective-permute-done((bf16[16,3072]{1,0:T(8,128)(2,1)S(1)}, bf16[16,3072]{1,0:T(8,128)(2,1)S(1)}, u32[]{:S(2)}, u32[]{:S(2)}) %collective-permute-start.15) | collective-permute-done | bytes 98336 | tf_op jit(solution)/shard_map/ppermute | solution.py:20
  54.9 0.6 collective-permute-done.17
  55.5 0.1 collective-permute-done.16
  55.7 0.1 fusion.8
  55.8 2.7 %collective-permute-start.18 = (bf16[4,6144]{1,0:T(4,128)(2,1)S(1)}, bf16[4,6144]{1,0:T(4,128)(2,1)S(1)}, u32[]{:S(2)}, u32[]{:S(2)}) collective-permute-start(bf16[4,6144]{1,0:T(4,128)(2,1)S(1)} %get-tuple-element.49), channel_id=1, source_target_pairs={{0,12},{1,13},{2,14},{3,15},{4,8},{5,9},{6,10},{7,11},{8,4},{9,5},... | collective-permute-start | bytes 147464 | tf_op jit(solution)/shard_map/ppermute | solution.py:20
  58.4 0.0 collective-permute-start.20
  58.4 1.8 %collective-permute-start.19 = (bf16[4,6144]{1,0:T(4,128)(2,1)S(1)}, bf16[4,6144]{1,0:T(4,128)(2,1)S(1)}, u32[]{:S(2)}, u32[]{:S(2)}) collective-permute-start(bf16[4,6144]{1,0:T(4,128)(2,1)S(1)} %get-tuple-element.51), channel_id=1, source_target_pairs={{0,8},{1,9},{2,10},{3,11},{4,12},{5,13},{6,14},{7,15},{8,0},{9,1},... | collective-permute-start | bytes 147464 | tf_op jit(solution)/shard_map/ppermute | solution.py:20
  60.2 1.6 %collective-permute-done.18 = bf16[4,6144]{1,0:T(4,128)(2,1)S(1)} collective-permute-done((bf16[4,6144]{1,0:T(4,128)(2,1)S(1)}, bf16[4,6144]{1,0:T(4,128)(2,1)S(1)}, u32[]{:S(2)}, u32[]{:S(2)}) %collective-permute-start.18) | collective-permute-done | bytes 49184 | tf_op jit(solution)/shard_map/ppermute | solution.py:20
  61.8 0.9 %collective-permute-done.20 = bf16[4,6144]{1,0:T(4,128)(2,1)S(1)} collective-permute-done((bf16[4,6144]{1,0:T(4,128)(2,1)S(1)}, bf16[4,6144]{1,0:T(4,128)(2,1)S(1)}, u32[]{:S(2)}, u32[]{:S(2)}) %collective-permute-start.20) | collective-permute-done | bytes 49184 | tf_op jit(solution)/shard_map/ppermute | solution.py:20
  62.7 0.7 %collective-permute-done.19 = bf16[4,6144]{1,0:T(4,128)(2,1)S(1)} collective-permute-done((bf16[4,6144]{1,0:T(4,128)(2,1)S(1)}, bf16[4,6144]{1,0:T(4,128)(2,1)S(1)}, u32[]{:S(2)}, u32[]{:S(2)}) %collective-permute-start.19) | collective-permute-done | bytes 49184 | tf_op jit(solution)/shard_map/ppermute | solution.py:20
  63.4 0.7 %fusion.3 = bf16[4,6144]{1,0:T(4,128)(2,1)} fusion(f32[16,3072]{1,0:T(8,128)S(1)} %slice_add_fusion.1, f32[16,3072]{1,0:T(8,128)S(1)} %slice_add_fusion, bf16[4,6144]{1,0:T(4,128)(2,1)S(1)} %collective-permute-done.20, bf16[4,6144]{1,0:T(4,128)(2,1)S(1)} %collective-permute-done.19, bf16[4,6144]{1,0:T(4,128)(2,1)S(1)} %collective-permute-done.18), kind=kLoop, calls=%fused_computation.11 | loop fusion | flops 196608 | bytes 589824 | tf_op jit(solution)/shard_map/convert_element_type | solution.py:287
  (5 shorter events, 0.2 us)
Async XLA Ops:
  0.9 10.3 %collective-permute-start.2 = (bf16[4,6272]{1,0:T(4,128)(2,1)S(1)}, bf16[4,6272]{1,0:T(4,128)(2,1)S(1)}, u32[]{:S(2)}, u32[]{:S(2)}) collective-permute-start(bf16[4,6272]{1,0:T(4,128)(2,1)S(1)} %shard_map.64.refs_2_), channel_id=1, source_target_pairs={{0,4},{1,5},{2,6},{3,7},{4,0},{5,1},{6,2},{7,3},{8,12},{9,13},{10,... | collective-permute-start | bytes 150536 | tf_op jit(solution)/shard_map/ppermute | solution.py:20
  4.0 7.2 %collective-permute-start.1 = (bf16[4,6272]{1,0:T(4,128)(2,1)S(1)}, bf16[4,6272]{1,0:T(4,128)(2,1)S(1)}, u32[]{:S(2)}, u32[]{:S(2)}) collective-permute-start(bf16[4,6272]{1,0:T(4,128)(2,1)S(1)} %shard_map.64.refs_2_), channel_id=1, source_target_pairs={{0,8},{1,9},{2,10},{3,11},{4,12},{5,13},{6,14},{7,15},{8,0},{9,1},... | collective-permute-start | bytes 150536 | tf_op jit(solution)/shard_map/ppermute | solution.py:20
  6.5 5.9 %collective-permute-start = (bf16[4,6272]{1,0:T(4,128)(2,1)S(1)}, bf16[4,6272]{1,0:T(4,128)(2,1)S(1)}, u32[]{:S(2)}, u32[]{:S(2)}) collective-permute-start(bf16[4,6272]{1,0:T(4,128)(2,1)S(1)} %shard_map.64.refs_2_), channel_id=1, source_target_pairs={{0,12},{1,13},{2,14},{3,15},{4,8},{5,9},{6,10},{7,11},{8,4},{9,5},... | collective-permute-start | bytes 150536 | tf_op jit(solution)/shard_map/ppermute | solution.py:20
  12.6 12.8 %collective-permute-start.3 = (bf16[16,6272]{1,0:T(8,128)(2,1)S(1)}, bf16[16,6272]{1,0:T(8,128)(2,1)S(1)}, u32[]{:S(2)}, u32[]{:S(2)}) collective-permute-start(bf16[16,6272]{1,0:T(8,128)(2,1)S(1)} %pad_maximum_fusion.1.refs_2_.refs_1_.refs_4_), channel_id=1, source_target_pairs={{0,2},{1,3},{2,0},{3,1},{4,6},{5,7},{6,4},{7,5},{8,10},{9,11},{10,... | collective-permute-start | bytes 602120 | tf_op jit(solution)/shard_map/ppermute | solution.py:20
  14.2 11.2 %collective-permute-start.5 = (bf16[16,6272]{1,0:T(8,128)(2,1)S(1)}, bf16[16,6272]{1,0:T(8,128)(2,1)S(1)}, u32[]{:S(2)}, u32[]{:S(2)}) collective-permute-start(bf16[16,6272]{1,0:T(8,128)(2,1)S(1)} %pad_maximum_fusion.1.refs_2_.refs_1_.refs_4_), channel_id=1, source_target_pairs={{0,16},{1,17},{2,18},{3,19},{4,20},{5,21},{6,22},{7,23},{8,24},{9,... | collective-permute-start | bytes 602120 | tf_op jit(solution)/shard_map/ppermute | solution.py:20
  15.6 10.3 %collective-permute-start.4 = (bf16[16,6272]{1,0:T(8,128)(2,1)S(1)}, bf16[16,6272]{1,0:T(8,128)(2,1)S(1)}, u32[]{:S(2)}, u32[]{:S(2)}) collective-permute-start(bf16[16,6272]{1,0:T(8,128)(2,1)S(1)} %pad_maximum_fusion.1.refs_2_.refs_1_.refs_4_), channel_id=1, source_target_pairs={{0,18},{1,19},{2,16},{3,17},{4,22},{5,23},{6,20},{7,21},{8,26},{9,... | collective-permute-start | bytes 602120 | tf_op jit(solution)/shard_map/ppermute | solution.py:20
  16.1 10.4 %collective-permute-start.6 = (bf16[16,6272]{1,0:T(8,128)(2,1)S(1)}, bf16[16,6272]{1,0:T(8,128)(2,1)S(1)}, u32[]{:S(2)}, u32[]{:S(2)}) collective-permute-start(bf16[16,6272]{1,0:T(8,128)(2,1)S(1)} %pad_maximum_fusion.1.refs_2_.refs_1_.refs_4_), channel_id=1, source_target_pairs={{0,1},{1,0},{2,3},{3,2},{4,5},{5,4},{6,7},{7,6},{8,9},{9,8},{10,11... | collective-permute-start | bytes 602120 | tf_op jit(solution)/shard_map/ppermute | solution.py:20
  25.4 2.3 %copy-start = (f32[8,128]{1,0:T(8,128)}, f32[8,128]{1,0:T(8,128)S(1)}, u32[]{:S(2)}) copy-start(f32[8,128]{1,0:T(8,128)S(1)} %get-tuple-element.27.refs_3_) | copy-start | bytes 12292
  25.4 1.6 %collective-permute-start.8 = (bf16[16,6272]{1,0:T(8,128)(2,1)S(1)}, bf16[16,6272]{1,0:T(8,128)(2,1)S(1)}, u32[]{:S(2)}, u32[]{:S(2)}) collective-permute-start(bf16[16,6272]{1,0:T(8,128)(2,1)S(1)} %collective-permute-done.5.refs_6_), channel_id=1, source_target_pairs={{0,1},{1,0},{2,3},{3,2},{4,5},{5,4},{6,7},{7,6},{8,9},{9,8},{10,11... | collective-permute-start | bytes 602120 | tf_op jit(solution)/shard_map/ppermute | solution.py:20
  26.0 1.4 %collective-permute-start.7 = (bf16[16,6272]{1,0:T(8,128)(2,1)S(1)}, bf16[16,6272]{1,0:T(8,128)(2,1)S(1)}, u32[]{:S(2)}, u32[]{:S(2)}) collective-permute-start(bf16[16,6272]{1,0:T(8,128)(2,1)S(1)} %collective-permute-done.4.refs_5_), channel_id=1, source_target_pairs={{0,1},{1,0},{2,3},{3,2},{4,5},{5,4},{6,7},{7,6},{8,9},{9,8},{10,11... | collective-permute-start | bytes 602120 | tf_op jit(solution)/shard_map/ppermute | solution.py:20
  26.1 1.6 %collective-permute-start.9 = (bf16[16,6272]{1,0:T(8,128)(2,1)S(1)}, bf16[16,6272]{1,0:T(8,128)(2,1)S(1)}, u32[]{:S(2)}, u32[]{:S(2)}) collective-permute-start(bf16[16,6272]{1,0:T(8,128)(2,1)S(1)} %collective-permute-done.3.refs_7_), channel_id=1, source_target_pairs={{0,1},{1,0},{2,3},{3,2},{4,5},{5,4},{6,7},{7,6},{8,9},{9,8},{10,11... | collective-permute-start | bytes 602120 | tf_op jit(solution)/shard_map/ppermute | solution.py:20
  41.4 1.8 %collective-permute-start.10 = (bf16[64,3072]{1,0:T(8,128)(2,1)S(1)}, bf16[64,3072]{1,0:T(8,128)(2,1)S(1)}, u32[]{:S(2)}, u32[]{:S(2)}) collective-permute-start(bf16[64,3072]{1,0:T(8,128)(2,1)S(1)} %get-tuple-element.36), channel_id=1, source_target_pairs={{0,1},{1,0},{2,3},{3,2},{4,5},{5,4},{6,7},{7,6},{8,9},{9,8},{10,11... | collective-permute-start | bytes 1179656 | tf_op jit(solution)/shard_map/ppermute | solution.py:20
  41.7 5.1 %collective-permute-start.14 = (bf16[64,3072]{1,0:T(8,128)(2,1)S(1)}, bf16[64,3072]{1,0:T(8,128)(2,1)S(1)}, u32[]{:S(2)}, u32[]{:S(2)}) collective-permute-start(bf16[64,3072]{1,0:T(8,128)(2,1)S(1)} %get-tuple-element.38), channel_id=1, source_target_pairs={{0,1},{1,0},{2,3},{3,2},{4,5},{5,4},{6,7},{7,6},{8,9},{9,8},{10,11... | collective-permute-start | bytes 1179656 | tf_op jit(solution)/shard_map/ppermute | solution.py:20
  43.3 6.7 %collective-permute-start.11 = (bf16[16,3072]{1,0:T(8,128)(2,1)S(1)}, bf16[16,3072]{1,0:T(8,128)(2,1)S(1)}, u32[]{:S(2)}, u32[]{:S(2)}) collective-permute-start(bf16[16,3072]{1,0:T(8,128)(2,1)S(1)} %get-tuple-element.46), channel_id=1, source_target_pairs={{0,18},{1,19},{2,16},{3,17},{4,22},{5,23},{6,20},{7,21},{8,26},{9,... | collective-permute-start | bytes 294920 | tf_op jit(solution)/shard_map/ppermute | solution.py:20
  45.8 6.7 %collective-permute-start.13 = (bf16[16,3072]{1,0:T(8,128)(2,1)S(1)}, bf16[16,3072]{1,0:T(8,128)(2,1)S(1)}, u32[]{:S(2)}, u32[]{:S(2)}) collective-permute-start(bf16[16,3072]{1,0:T(8,128)(2,1)S(1)} %get-tuple-element.47), channel_id=1, source_target_pairs={{0,2},{1,3},{2,0},{3,1},{4,6},{5,7},{6,4},{7,5},{8,10},{9,11},{10,... | collective-permute-start | bytes 294920 | tf_op jit(solution)/shard_map/ppermute | solution.py:20
  46.3 6.2 %collective-permute-start.12 = (bf16[16,3072]{1,0:T(8,128)(2,1)S(1)}, bf16[16,3072]{1,0:T(8,128)(2,1)S(1)}, u32[]{:S(2)}, u32[]{:S(2)}) collective-permute-start(bf16[16,3072]{1,0:T(8,128)(2,1)S(1)} %get-tuple-element.48), channel_id=1, source_target_pairs={{0,16},{1,17},{2,18},{3,19},{4,20},{5,21},{6,22},{7,23},{8,24},{9,... | collective-permute-start | bytes 294920 | tf_op jit(solution)/shard_map/ppermute | solution.py:20
  47.0 8.0 %collective-permute-start.15 = (bf16[16,3072]{1,0:T(8,128)(2,1)S(1)}, bf16[16,3072]{1,0:T(8,128)(2,1)S(1)}, u32[]{:S(2)}, u32[]{:S(2)}) collective-permute-start(bf16[16,3072]{1,0:T(8,128)(2,1)S(1)} %get-tuple-element.43), channel_id=1, source_target_pairs={{0,18},{1,19},{2,16},{3,17},{4,22},{5,23},{6,20},{7,21},{8,26},{9,... | collective-permute-start | bytes 294920 | tf_op jit(solution)/shard_map/ppermute | solution.py:20
  49.5 6.0 %collective-permute-start.17 = (bf16[16,3072]{1,0:T(8,128)(2,1)S(1)}, bf16[16,3072]{1,0:T(8,128)(2,1)S(1)}, u32[]{:S(2)}, u32[]{:S(2)}) collective-permute-start(bf16[16,3072]{1,0:T(8,128)(2,1)S(1)} %get-tuple-element.44), channel_id=1, source_target_pairs={{0,2},{1,3},{2,0},{3,1},{4,6},{5,7},{6,4},{7,5},{8,10},{9,11},{10,... | collective-permute-start | bytes 294920 | tf_op jit(solution)/shard_map/ppermute | solution.py:20
  50.0 5.6 %collective-permute-start.16 = (bf16[16,3072]{1,0:T(8,128)(2,1)S(1)}, bf16[16,3072]{1,0:T(8,128)(2,1)S(1)}, u32[]{:S(2)}, u32[]{:S(2)}) collective-permute-start(bf16[16,3072]{1,0:T(8,128)(2,1)S(1)} %get-tuple-element.45), channel_id=1, source_target_pairs={{0,16},{1,17},{2,18},{3,19},{4,20},{5,21},{6,22},{7,23},{8,24},{9,... | collective-permute-start | bytes 294920 | tf_op jit(solution)/shard_map/ppermute | solution.py:20
  55.8 6.1 %collective-permute-start.18 = (bf16[4,6144]{1,0:T(4,128)(2,1)S(1)}, bf16[4,6144]{1,0:T(4,128)(2,1)S(1)}, u32[]{:S(2)}, u32[]{:S(2)}) collective-permute-start(bf16[4,6144]{1,0:T(4,128)(2,1)S(1)} %get-tuple-element.49), channel_id=1, source_target_pairs={{0,12},{1,13},{2,14},{3,15},{4,8},{5,9},{6,10},{7,11},{8,4},{9,5},... | collective-permute-start | bytes 147464 | tf_op jit(solution)/shard_map/ppermute | solution.py:20
  58.4 4.3 %collective-permute-start.20 = (bf16[4,6144]{1,0:T(4,128)(2,1)S(1)}, bf16[4,6144]{1,0:T(4,128)(2,1)S(1)}, u32[]{:S(2)}, u32[]{:S(2)}) collective-permute-start(bf16[4,6144]{1,0:T(4,128)(2,1)S(1)} %get-tuple-element.50), channel_id=1, source_target_pairs={{0,4},{1,5},{2,6},{3,7},{4,0},{5,1},{6,2},{7,3},{8,12},{9,13},{10,... | collective-permute-start | bytes 147464 | tf_op jit(solution)/shard_map/ppermute | solution.py:20
  58.4 5.0 %collective-permute-start.19 = (bf16[4,6144]{1,0:T(4,128)(2,1)S(1)}, bf16[4,6144]{1,0:T(4,128)(2,1)S(1)}, u32[]{:S(2)}, u32[]{:S(2)}) collective-permute-start(bf16[4,6144]{1,0:T(4,128)(2,1)S(1)} %get-tuple-element.51), channel_id=1, source_target_pairs={{0,8},{1,9},{2,10},{3,11},{4,12},{5,13},{6,14},{7,15},{8,0},{9,1},... | collective-permute-start | bytes 147464 | tf_op jit(solution)/shard_map/ppermute | solution.py:20
